TPU v7x, 32 devices: a whole 2x2x4 slice. The times are simulated.
32 devices in a mesh: gx: 4 (over x, core), gy: 8 (over z, y).
Axes of the slice: x: 2, y: 2, z: 4, core: 2. Of those that a mesh axis runs over, the one named last changes fastest.
Arguments:
- solution: float32 [32, 64, 512], P('gx', 'gy'), may hold values from -6 to 6
- right_side: float32 [32, 64, 512], P('gx', 'gy'), may hold values from -6 to 6
- alpha: bfloat16 [32, 64, 512], P('gx', 'gy'), may hold values from 0.5 to 2
- beta_x: bfloat16 [32, 64, 512], P('gx', 'gy'), may hold values from 0.25 to 2.5
- beta_y: bfloat16 [32, 64, 512], P('gx', 'gy'), may hold values from 0.25 to 2.5
- beta_z: bfloat16 [32, 64, 512], P('gx', 'gy'), may hold values from 0.25 to 2.5
Outputs:
- fine_iterate: float32 [32, 64, 512], P('gx', 'gy')
- middle_iterate: float32 [16, 32, 256], P('gx', 'gy')
- coarse_iterate: float32 [8, 16, 128], P('gx', 'gy')
All inputs are finite; a program needn't handle non-finite values.
Results may differ from a plain program's by a relative error of at most 0.0003.
Values sent between devices are 32-bit elements; how exact they have to be, the bound alone decides.
A program may use at most 64 MiB of HBM per device.

v0:
```python
import jax
import jax.numpy as jnp
from jax import lax
from jax.sharding import PartitionSpec as P

LEVELS = 3
SWEEPS = 2


def from_behind(block, axis, distance):
    devices = range(lax.axis_size(axis))
    route = [(i - distance, i) for i in devices if i - distance in devices]
    return lax.ppermute(block, axis, route)


def padded_2(shard, sides, width):
    for axis, dim in sides:
        count, length = (lax.axis_size(axis), shard.shape[dim])
        up = [(i, (i + 1) % count) for i in range(count - 1)]
        down = [(j, i) for i, j in up]
        last = lax.slice_in_dim(shard, length - width, length, axis=dim)
        first = lax.slice_in_dim(shard, 0, width, axis=dim)
        before = lax.ppermute(last, axis, up)
        after = lax.ppermute(first, axis, down)
        shard = jnp.concatenate([before, shard, after], axis=dim)
    return shard


def shift_up(field, axis):
    size = field.shape[axis]
    rest = lax.slice_in_dim(field, 1, size, axis=axis)
    edge = jnp.zeros_like(lax.slice_in_dim(field, 0, 1, axis=axis))
    return jnp.concatenate([rest, edge], axis=axis)


def shift_down(field, axis):
    size = field.shape[axis]
    rest = lax.slice_in_dim(field, 0, size - 1, axis=axis)
    edge = jnp.zeros_like(lax.slice_in_dim(field, 0, 1, axis=axis))
    return jnp.concatenate([edge, rest], axis=axis)


def stencil(field, beside, coefs, scale):
    out = coefs[0] * field
    for direc in range(3):
        upper_face = coefs[1 + 2 * direc]
        lower_face = coefs[2 + 2 * direc]
        out = out + scale * (
            upper_face * (field - beside[2 * direc]) + lower_face * (field - beside[2 * direc + 1])
        )
    return out


def diagonal_of(coefs, scale):
    return coefs[0] + scale * (coefs[1] + coefs[2] + (coefs[3] + coefs[4]) + (coefs[5] + coefs[6]))


def parity_of(shape):
    total = (
        lax.broadcasted_iota(jnp.int32, shape, 0)
        + lax.broadcasted_iota(jnp.int32, shape, 1)
        + lax.broadcasted_iota(jnp.int32, shape, 2)
    )
    return total % 2


def coarsen_cells(field):
    nx, ny, nz = field.shape
    return field.reshape(nx // 2, 2, ny // 2, 2, nz // 2, 2).mean(axis=(1, 3, 5))


def coarsen_faces(bx, by, bz):
    nx, ny, nz = bx.shape
    cx = bx[1::2].reshape(nx // 2, ny // 2, 2, nz // 2, 2).mean(axis=(2, 4))
    cy = by[:, 1::2].reshape(nx // 2, 2, ny // 2, nz // 2, 2).mean(axis=(1, 4))
    cz = bz[:, :, 1::2].reshape(nx // 2, 2, ny // 2, 2, nz // 2).mean(axis=(1, 3))
    return (cx, cy, cz)


def from_x(layer, stride):
    return from_behind(layer, "gx", stride)


def from_y(layer, stride):
    return from_behind(layer, "gy", stride)


def neighbours(field):
    padded = padded_2(field, (("gx", 0), ("gy", 1)), 1)
    return (
        padded[2:, 1:-1],
        padded[:-2, 1:-1],
        padded[1:-1, 2:],
        padded[1:-1, :-2],
        shift_up(field, 2),
        shift_down(field, 2),
    )


def lower_faces(face_x, face_y, face_z, group):
    edge_x = from_x(face_x[-1:], group)
    edge_y = from_y(face_y[:, -1:], group)
    below_x = jnp.concatenate([edge_x, face_x[:-1]], axis=0)
    below_y = jnp.concatenate([edge_y, face_y[:, :-1]], axis=1)
    return (below_x, below_y, shift_down(face_z, 2))


def shards(solution, right_side, alpha, beta_x, beta_y, beta_z):
    iterate = solution
    source = right_side
    cell_coef = alpha.astype(jnp.float32)
    face_x = beta_x.astype(jnp.float32)
    face_y = beta_y.astype(jnp.float32)
    face_z = beta_z.astype(jnp.float32)
    results = []
    for level in range(LEVELS):
        scale = 0.25**level
        group = 1
        below_x, below_y, below_z = lower_faces(face_x, face_y, face_z, group)
        coefs = (cell_coef, face_x, below_x, face_y, below_y, face_z, below_z)
        diag = diagonal_of(coefs, scale)
        parity = parity_of(iterate.shape)
        for sweep in range(SWEEPS):
            for colour in (0, 1):
                resid = source - stencil(iterate, neighbours(iterate), coefs, scale)
                iterate = jnp.where(parity == colour, iterate + resid / diag, iterate)
        results.append(iterate)
        if level + 1 < LEVELS:
            resid = source - stencil(iterate, neighbours(iterate), coefs, scale)
            source = coarsen_cells(resid)
            cell_coef = coarsen_cells(cell_coef)
            face_x, face_y, face_z = coarsen_faces(face_x, face_y, face_z)
            iterate = jnp.zeros_like(source)
    return (results[0], results[1], results[2])


def solution(mesh):
    placed = (
        P("gx", "gy", None),
        P("gx", "gy", None),
        P("gx", "gy", None),
        P("gx", "gy", None),
        P("gx", "gy", None),
        P("gx", "gy", None),
    )
    return jax.shard_map(
        shards,
        mesh=mesh,
        in_specs=placed,
        out_specs=(P("gx", "gy", None), P("gx", "gy", None), P("gx", "gy", None)),
        check_vma=False,
    )
```

profile of v0, /device:TPU:26, one launch (start us, length us, event | category | flops | bytes accessed | tf_op | source)
XLA Modules:
  0.0 263.7 jit_solution(3667122242642801014)
XLA Ops:
  3.3 3.6 %collective-permute-start = (f32[1,8,512]{2,1,0:T(8,128)S(1)}, f32[1,8,512]{2,1,0:T(8,128)S(1)}, u32[]{:S(2)}, u32[]{:S(2)}) collective-permute-start(f32[1,8,512]{2,1,0:T(8,128)S(1)} %get-tuple-element.37), channel_id=1, source_target_pairs={{8,0},{16,8},{24,16},{9,1},{17,9},{25,17},{10,2},{18,10},{26,18},{... | collective-permute-start | bytes 49160 | tf_op jit(solution)/shard_map/ppermute | solution.py:24
  10.5 3.4 %collective-permute-start.4 = (f32[8,1,512]{2,1,0:T(1,128)S(1)}, f32[8,1,512]{2,1,0:T(1,128)S(1)}, u32[]{:S(2)}, u32[]{:S(2)}) collective-permute-start(f32[8,1,512]{2,1,0:T(1,128)S(1)} %slice.671), channel_id=1, source_target_pairs={{0,1},{1,2},{2,3},{3,4},{4,5},{5,6},{6,7},{8,9},{9,10},{10,11},{11... | collective-permute-start | bytes 49160 | tf_op jit(solution)/shard_map/ppermute | solution.py:13
  13.9 3.4 %collective-permute-start.22 = (f32[1,4,256]{2,1,0:T(4,128)S(1)}, f32[1,4,256]{2,1,0:T(4,128)S(1)}, u32[]{:S(2)}, u32[]{:S(2)}) collective-permute-start(f32[1,4,256]{2,1,0:T(4,128)S(1)} %broadcast.134), channel_id=1, source_target_pairs={{8,0},{16,8},{24,16},{9,1},{17,9},{25,17},{10,2},{18,10},{26,18},{... | collective-permute-start | bytes 12296 | tf_op jit(solution)/shard_map/ppermute | solution.py:24
  26.5 9.7 %reshape.38 = f32[4,2,4,2,256,2]{5,4,3,2,1,0:T(8,128)} reshape(bf16[8,8,512]{2,1,0:T(8,128)(2,1)S(1)} %copy-done.6) | data formatting | bytes 196608 | tf_op jit(solution)/shard_map/reshape | solution.py:69
  36.2 4.0 %reduce_sum.91 = f32[4,4,256]{2,1,0:T(4,128)S(1)} reduce(f32[4,2,4,2,256,2]{5,4,3,2,1,0:T(8,128)} %reshape.38, f32[]{:T(128)} %constant.65.clone.1), dimensions={1,3,5}, to_apply=%region_1.2 | reduce | flops 28672 | bytes 147460 | tf_op jit(solution)/shard_map/reduce_sum | solution.py:69
  40.3 3.3 %collective-permute-start.3 = (f32[10,1,512]{2,1,0:T(1,128)S(1)}, f32[10,1,512]{2,1,0:T(1,128)S(1)}, u32[]{:S(2)}, u32[]{:S(2)}) collective-permute-start(f32[10,1,512]{2,1,0:T(1,128)S(1)} %get-tuple-element.17), channel_id=1, source_target_pairs={{1,0},{2,1},{3,2},{4,3},{5,4},{6,5},{7,6},{9,8},{10,9},{11,10},{12... | collective-permute-start | bytes 61448 | tf_op jit(solution)/shard_map/ppermute | solution.py:24
  51.1 3.6 %collective-permute-start.6 = (f32[1,8,512]{2,1,0:T(8,128)S(1)}, f32[1,8,512]{2,1,0:T(8,128)S(1)}, u32[]{:S(2)}, u32[]{:S(2)}) collective-permute-start(f32[1,8,512]{2,1,0:T(8,128)S(1)} %get-tuple-element.34), channel_id=1, source_target_pairs={{8,0},{16,8},{24,16},{9,1},{17,9},{25,17},{10,2},{18,10},{26,18},{... | collective-permute-start | bytes 49160 | tf_op jit(solution)/shard_map/ppermute | solution.py:24
  59.8 4.2 %collective-permute-start.8 = (f32[10,1,512]{2,1,0:T(1,128)S(1)}, f32[10,1,512]{2,1,0:T(1,128)S(1)}, u32[]{:S(2)}, u32[]{:S(2)}) collective-permute-start(f32[10,1,512]{2,1,0:T(1,128)S(1)} %get-tuple-element.15), channel_id=1, source_target_pairs={{1,0},{2,1},{3,2},{4,3},{5,4},{6,5},{7,6},{9,8},{10,9},{11,10},{12... | collective-permute-start | bytes 61448 | tf_op jit(solution)/shard_map/ppermute | solution.py:24
  66.1 4.5 %collective-permute-done.9 = f32[10,1,512]{2,1,0:T(1,128)S(1)} collective-permute-done((f32[10,1,512]{2,1,0:T(1,128)S(1)}, f32[10,1,512]{2,1,0:T(1,128)S(1)}, u32[]{:S(2)}, u32[]{:S(2)}) %collective-permute-start.9) | collective-permute-done | bytes 20512 | tf_op jit(solution)/shard_map/ppermute | solution.py:23
  79.8 3.9 %collective-permute-start.13 = (f32[10,1,512]{2,1,0:T(1,128)S(1)}, f32[10,1,512]{2,1,0:T(1,128)S(1)}, u32[]{:S(2)}, u32[]{:S(2)}) collective-permute-start(f32[10,1,512]{2,1,0:T(1,128)S(1)} %get-tuple-element.14), channel_id=1, source_target_pairs={{0,1},{1,2},{2,3},{3,4},{4,5},{5,6},{6,7},{8,9},{9,10},{10,11},{11... | collective-permute-start | bytes 61448 | tf_op jit(solution)/shard_map/ppermute | solution.py:23
  118.5 4.1 %collective-permute-start.25 = (f32[6,1,256]{2,1,0:T(1,128)S(1)}, f32[6,1,256]{2,1,0:T(1,128)S(1)}, u32[]{:S(2)}, u32[]{:S(2)}) collective-permute-start(f32[6,1,256]{2,1,0:T(1,128)S(1)} %get-tuple-element.47), channel_id=1, source_target_pairs={{1,0},{2,1},{3,2},{4,3},{5,4},{6,5},{7,6},{9,8},{10,9},{11,10},{12... | collective-permute-start | bytes 18440 | tf_op jit(solution)/shard_map/ppermute | solution.py:24
  124.9 9.8 %reshape.37 = f32[4,2,4,2,256,2]{5,4,3,2,1,0:T(8,128)} reshape(f32[8,8,512]{2,1,0:T(8,128)S(1)} %fusion.24) | data formatting | bytes 262144 | tf_op jit(solution)/shard_map/reshape | solution.py:69
  134.7 4.0 %reduce_sum.90 = f32[4,4,256]{2,1,0:T(4,128)S(1)} reduce(f32[4,2,4,2,256,2]{5,4,3,2,1,0:T(8,128)} %reshape.37, f32[]{:T(128)} %constant.65.clone.1), dimensions={1,3,5}, to_apply=%region_0.1 | reduce | flops 28672 | bytes 147460 | tf_op jit(solution)/shard_map/reduce_sum | solution.py:69
  142.7 3.6 %collective-permute-start.28 = (f32[1,4,256]{2,1,0:T(4,128)S(1)}, f32[1,4,256]{2,1,0:T(4,128)S(1)}, u32[]{:S(2)}, u32[]{:S(2)}) collective-permute-start(f32[1,4,256]{2,1,0:T(4,128)S(1)} %get-tuple-element.64), channel_id=1, source_target_pairs={{8,0},{16,8},{24,16},{9,1},{17,9},{25,17},{10,2},{18,10},{26,18},{... | collective-permute-start | bytes 12296 | tf_op jit(solution)/shard_map/ppermute | solution.py:24
  151.3 4.8 %collective-permute-start.30 = (f32[6,1,256]{2,1,0:T(1,128)S(1)}, f32[6,1,256]{2,1,0:T(1,128)S(1)}, u32[]{:S(2)}, u32[]{:S(2)}) collective-permute-start(f32[6,1,256]{2,1,0:T(1,128)S(1)} %get-tuple-element.45), channel_id=1, source_target_pairs={{1,0},{2,1},{3,2},{4,3},{5,4},{6,5},{7,6},{9,8},{10,9},{11,10},{12... | collective-permute-start | bytes 18440 | tf_op jit(solution)/shard_map/ppermute | solution.py:24
  158.2 4.4 %collective-permute-done.31 = f32[6,1,256]{2,1,0:T(1,128)S(1)} collective-permute-done((f32[6,1,256]{2,1,0:T(1,128)S(1)}, f32[6,1,256]{2,1,0:T(1,128)S(1)}, u32[]{:S(2)}, u32[]{:S(2)}) %collective-permute-start.31) | collective-permute-done | bytes 6176 | tf_op jit(solution)/shard_map/ppermute | solution.py:23
  171.5 3.9 %collective-permute-start.35 = (f32[6,1,256]{2,1,0:T(1,128)S(1)}, f32[6,1,256]{2,1,0:T(1,128)S(1)}, u32[]{:S(2)}, u32[]{:S(2)}) collective-permute-start(f32[6,1,256]{2,1,0:T(1,128)S(1)} %get-tuple-element.44), channel_id=1, source_target_pairs={{0,1},{1,2},{2,3},{3,4},{4,5},{5,6},{6,7},{8,9},{9,10},{10,11},{11... | collective-permute-start | bytes 18440 | tf_op jit(solution)/shard_map/ppermute | solution.py:23
  184.9 4.3 %collective-permute-start.38 = (f32[6,1,256]{2,1,0:T(1,128)S(1)}, f32[6,1,256]{2,1,0:T(1,128)S(1)}, u32[]{:S(2)}, u32[]{:S(2)}) collective-permute-start(f32[6,1,256]{2,1,0:T(1,128)S(1)} %get-tuple-element.41), channel_id=1, source_target_pairs={{1,0},{2,1},{3,2},{4,3},{5,4},{6,5},{7,6},{9,8},{10,9},{11,10},{12... | collective-permute-start | bytes 18440 | tf_op jit(solution)/shard_map/ppermute | solution.py:24
  191.3 4.4 %collective-permute-done.39 = f32[6,1,256]{2,1,0:T(1,128)S(1)} collective-permute-done((f32[6,1,256]{2,1,0:T(1,128)S(1)}, f32[6,1,256]{2,1,0:T(1,128)S(1)}, u32[]{:S(2)}, u32[]{:S(2)}) %collective-permute-start.39) | collective-permute-done | bytes 6176 | tf_op jit(solution)/shard_map/ppermute | solution.py:23
  202.7 3.3 %collective-permute-start.42 = (f32[6,1,256]{2,1,0:T(1,128)S(1)}, f32[6,1,256]{2,1,0:T(1,128)S(1)}, u32[]{:S(2)}, u32[]{:S(2)}) collective-permute-start(f32[6,1,256]{2,1,0:T(1,128)S(1)} %get-tuple-element.39), channel_id=1, source_target_pairs={{1,0},{2,1},{3,2},{4,3},{5,4},{6,5},{7,6},{9,8},{10,9},{11,10},{12... | collective-permute-start | bytes 18440 | tf_op jit(solution)/shard_map/ppermute | solution.py:24
  221.9 3.3 %collective-permute-start.52 = (f32[4,1,128]{2,1,0:T(1,128)S(1)}, f32[4,1,128]{2,1,0:T(1,128)S(1)}, u32[]{:S(2)}, u32[]{:S(2)}) collective-permute-start(f32[4,1,128]{2,1,0:T(1,128)S(1)} %get-tuple-element.69), channel_id=1, source_target_pairs={{1,0},{2,1},{3,2},{4,3},{5,4},{6,5},{7,6},{9,8},{10,9},{11,10},{12... | collective-permute-start | bytes 6152 | tf_op jit(solution)/shard_map/ppermute | solution.py:24
  227.8 3.7 %collective-permute-done.53 = f32[4,1,128]{2,1,0:T(1,128)S(1)} collective-permute-done((f32[4,1,128]{2,1,0:T(1,128)S(1)}, f32[4,1,128]{2,1,0:T(1,128)S(1)}, u32[]{:S(2)}, u32[]{:S(2)}) %collective-permute-start.53) | collective-permute-done | bytes 2080 | tf_op jit(solution)/shard_map/ppermute | solution.py:23
  240.4 3.9 %collective-permute-start.57 = (f32[4,1,128]{2,1,0:T(1,128)S(1)}, f32[4,1,128]{2,1,0:T(1,128)S(1)}, u32[]{:S(2)}, u32[]{:S(2)}) collective-permute-start(f32[4,1,128]{2,1,0:T(1,128)S(1)} %get-tuple-element.68), channel_id=1, source_target_pairs={{0,1},{1,2},{2,3},{3,4},{4,5},{5,6},{6,7},{8,9},{9,10},{10,11},{11... | collective-permute-start | bytes 6152 | tf_op jit(solution)/shard_map/ppermute | solution.py:23
  259.6 3.4 %collective-permute-done.61 = f32[4,1,128]{2,1,0:T(1,128)S(1)} collective-permute-done((f32[4,1,128]{2,1,0:T(1,128)S(1)}, f32[4,1,128]{2,1,0:T(1,128)S(1)}, u32[]{:S(2)}, u32[]{:S(2)}) %collective-permute-start.61) | collective-permute-done | bytes 2080 | tf_op jit(solution)/shard_map/ppermute | solution.py:23
  (223 shorter events, 156.9 us)
Async XLA Ops:
  1.4 38.8 %collective-permute-start.2 = (f32[1,8,512]{2,1,0:T(8,128)S(1)}, f32[1,8,512]{2,1,0:T(8,128)S(1)}, u32[]{:S(2)}, u32[]{:S(2)}) collective-permute-start(f32[1,8,512]{2,1,0:T(8,128)S(1)} %get-tuple-element.38), channel_id=1, source_target_pairs={{0,8},{8,16},{16,24},{1,9},{9,17},{17,25},{2,10},{10,18},{18,26},{... | collective-permute-start | bytes 49160 | tf_op jit(solution)/shard_map/ppermute | solution.py:23
  3.3 36.9 %collective-permute-start = (f32[1,8,512]{2,1,0:T(8,128)S(1)}, f32[1,8,512]{2,1,0:T(8,128)S(1)}, u32[]{:S(2)}, u32[]{:S(2)}) collective-permute-start(f32[1,8,512]{2,1,0:T(8,128)S(1)} %get-tuple-element.37), channel_id=1, source_target_pairs={{8,0},{16,8},{24,16},{9,1},{17,9},{25,17},{10,2},{18,10},{26,18},{... | collective-permute-start | bytes 49160 | tf_op jit(solution)/shard_map/ppermute | solution.py:24
  7.7 39.2 %collective-permute-start.1 = (f32[1,8,512]{2,1,0:T(8,128)S(1)}, f32[1,8,512]{2,1,0:T(8,128)S(1)}, u32[]{:S(2)}, u32[]{:S(2)}) collective-permute-start(f32[1,8,512]{2,1,0:T(8,128)S(1)} %slice.668), channel_id=1, source_target_pairs={{0,8},{8,16},{16,24},{1,9},{9,17},{17,25},{2,10},{10,18},{18,26},{... | collective-permute-start | bytes 49160 | tf_op jit(solution)/shard_map/ppermute | solution.py:13
  10.5 38.4 %collective-permute-start.4 = (f32[8,1,512]{2,1,0:T(1,128)S(1)}, f32[8,1,512]{2,1,0:T(1,128)S(1)}, u32[]{:S(2)}, u32[]{:S(2)}) collective-permute-start(f32[8,1,512]{2,1,0:T(1,128)S(1)} %slice.671), channel_id=1, source_target_pairs={{0,1},{1,2},{2,3},{3,4},{4,5},{5,6},{6,7},{8,9},{9,10},{10,11},{11... | collective-permute-start | bytes 49160 | tf_op jit(solution)/shard_map/ppermute | solution.py:13
  13.9 91.5 %collective-permute-start.22 = (f32[1,4,256]{2,1,0:T(4,128)S(1)}, f32[1,4,256]{2,1,0:T(4,128)S(1)}, u32[]{:S(2)}, u32[]{:S(2)}) collective-permute-start(f32[1,4,256]{2,1,0:T(4,128)S(1)} %broadcast.134), channel_id=1, source_target_pairs={{8,0},{16,8},{24,16},{9,1},{17,9},{25,17},{10,2},{18,10},{26,18},{... | collective-permute-start | bytes 12296 | tf_op jit(solution)/shard_map/ppermute | solution.py:24
  40.3 10.5 %collective-permute-start.3 = (f32[10,1,512]{2,1,0:T(1,128)S(1)}, f32[10,1,512]{2,1,0:T(1,128)S(1)}, u32[]{:S(2)}, u32[]{:S(2)}) collective-permute-start(f32[10,1,512]{2,1,0:T(1,128)S(1)} %get-tuple-element.17), channel_id=1, source_target_pairs={{1,0},{2,1},{3,2},{4,3},{5,4},{6,5},{7,6},{9,8},{10,9},{11,10},{12... | collective-permute-start | bytes 61448 | tf_op jit(solution)/shard_map/ppermute | solution.py:24
  43.6 7.2 %collective-permute-start.5 = (f32[10,1,512]{2,1,0:T(1,128)S(1)}, f32[10,1,512]{2,1,0:T(1,128)S(1)}, u32[]{:S(2)}, u32[]{:S(2)}) collective-permute-start(f32[10,1,512]{2,1,0:T(1,128)S(1)} %get-tuple-element.18), channel_id=1, source_target_pairs={{0,1},{1,2},{2,3},{3,4},{4,5},{5,6},{6,7},{8,9},{9,10},{10,11},{11... | collective-permute-start | bytes 61448 | tf_op jit(solution)/shard_map/ppermute | solution.py:23
  46.9 60.5 %collective-permute-start.24 = (f32[1,4,256]{2,1,0:T(4,128)S(1)}, f32[1,4,256]{2,1,0:T(4,128)S(1)}, u32[]{:S(2)}, u32[]{:S(2)}) collective-permute-start(f32[1,4,256]{2,1,0:T(4,128)S(1)} %broadcast.134), channel_id=1, source_target_pairs={{0,8},{8,16},{16,24},{1,9},{9,17},{17,25},{2,10},{10,18},{18,26},{... | collective-permute-start | bytes 12296 | tf_op jit(solution)/shard_map/ppermute | solution.py:23
  48.9 89.9 %collective-permute-start.23 = (f32[1,4,256]{2,1,0:T(4,128)S(1)}, f32[1,4,256]{2,1,0:T(4,128)S(1)}, u32[]{:S(2)}, u32[]{:S(2)}) collective-permute-start(f32[1,4,256]{2,1,0:T(4,128)S(1)} %slice.691), channel_id=1, source_target_pairs={{0,8},{8,16},{16,24},{1,9},{9,17},{17,25},{2,10},{10,18},{18,26},{... | collective-permute-start | bytes 12296 | tf_op jit(solution)/shard_map/ppermute | solution.py:13
  64.1 6.6 %collective-permute-start.9 = (f32[10,1,512]{2,1,0:T(1,128)S(1)}, f32[10,1,512]{2,1,0:T(1,128)S(1)}, u32[]{:S(2)}, u32[]{:S(2)}) collective-permute-start(f32[10,1,512]{2,1,0:T(1,128)S(1)} %get-tuple-element.16), channel_id=1, source_target_pairs={{0,1},{1,2},{2,3},{3,4},{4,5},{5,6},{6,7},{8,9},{9,10},{10,11},{11... | collective-permute-start | bytes 61448 | tf_op jit(solution)/shard_map/ppermute | solution.py:23
  79.8 6.6 %collective-permute-start.13 = (f32[10,1,512]{2,1,0:T(1,128)S(1)}, f32[10,1,512]{2,1,0:T(1,128)S(1)}, u32[]{:S(2)}, u32[]{:S(2)}) collective-permute-start(f32[10,1,512]{2,1,0:T(1,128)S(1)} %get-tuple-element.14), channel_id=1, source_target_pairs={{0,1},{1,2},{2,3},{3,4},{4,5},{5,6},{6,7},{8,9},{9,10},{10,11},{11... | collective-permute-start | bytes 61448 | tf_op jit(solution)/shard_map/ppermute | solution.py:23
  96.6 6.6 %collective-permute-start.17 = (f32[10,1,512]{2,1,0:T(1,128)S(1)}, f32[10,1,512]{2,1,0:T(1,128)S(1)}, u32[]{:S(2)}, u32[]{:S(2)}) collective-permute-start(f32[10,1,512]{2,1,0:T(1,128)S(1)} %get-tuple-element.12), channel_id=1, source_target_pairs={{0,1},{1,2},{2,3},{3,4},{4,5},{5,6},{6,7},{8,9},{9,10},{10,11},{11... | collective-permute-start | bytes 61448 | tf_op jit(solution)/shard_map/ppermute | solution.py:23
  99.7 41.0 %collective-permute-start.26 = (f32[4,1,256]{2,1,0:T(1,128)S(1)}, f32[4,1,256]{2,1,0:T(1,128)S(1)}, u32[]{:S(2)}, u32[]{:S(2)}) collective-permute-start(f32[4,1,256]{2,1,0:T(1,128)S(1)} %slice.693), channel_id=1, source_target_pairs={{0,1},{1,2},{2,3},{3,4},{4,5},{5,6},{6,7},{8,9},{9,10},{10,11},{11... | collective-permute-start | bytes 12296 | tf_op jit(solution)/shard_map/ppermute | solution.py:13
  103.3 76.7 %collective-permute-start.44 = (f32[1,2,128]{2,1,0:T(2,128)S(1)}, f32[1,2,128]{2,1,0:T(2,128)S(1)}, u32[]{:S(2)}, u32[]{:S(2)}) collective-permute-start(f32[1,2,128]{2,1,0:T(2,128)S(1)} %broadcast.138), channel_id=1, source_target_pairs={{8,0},{16,8},{24,16},{9,1},{17,9},{25,17},{10,2},{18,10},{26,18},{... | collective-permute-start | bytes 3080 | tf_op jit(solution)/shard_map/ppermute | solution.py:24
  115.7 6.9 %collective-permute-start.21 = (f32[10,1,512]{2,1,0:T(1,128)S(1)}, f32[10,1,512]{2,1,0:T(1,128)S(1)}, u32[]{:S(2)}, u32[]{:S(2)}) collective-permute-start(f32[10,1,512]{2,1,0:T(1,128)S(1)} %get-tuple-element.10), channel_id=1, source_target_pairs={{0,1},{1,2},{2,3},{3,4},{4,5},{5,6},{6,7},{8,9},{9,10},{10,11},{11... | collective-permute-start | bytes 61448 | tf_op jit(solution)/shard_map/ppermute | solution.py:23
  118.5 24.1 %collective-permute-start.25 = (f32[6,1,256]{2,1,0:T(1,128)S(1)}, f32[6,1,256]{2,1,0:T(1,128)S(1)}, u32[]{:S(2)}, u32[]{:S(2)}) collective-permute-start(f32[6,1,256]{2,1,0:T(1,128)S(1)} %get-tuple-element.47), channel_id=1, source_target_pairs={{1,0},{2,1},{3,2},{4,3},{5,4},{6,5},{7,6},{9,8},{10,9},{11,10},{12... | collective-permute-start | bytes 18440 | tf_op jit(solution)/shard_map/ppermute | solution.py:24
  122.6 20.0 %collective-permute-start.27 = (f32[6,1,256]{2,1,0:T(1,128)S(1)}, f32[6,1,256]{2,1,0:T(1,128)S(1)}, u32[]{:S(2)}, u32[]{:S(2)}) collective-permute-start(f32[6,1,256]{2,1,0:T(1,128)S(1)} %get-tuple-element.48), channel_id=1, source_target_pairs={{0,1},{1,2},{2,3},{3,4},{4,5},{5,6},{6,7},{8,9},{9,10},{10,11},{11... | collective-permute-start | bytes 18440 | tf_op jit(solution)/shard_map/ppermute | solution.py:23
  138.7 43.6 %collective-permute-start.46 = (f32[1,2,128]{2,1,0:T(2,128)S(1)}, f32[1,2,128]{2,1,0:T(2,128)S(1)}, u32[]{:S(2)}, u32[]{:S(2)}) collective-permute-start(f32[1,2,128]{2,1,0:T(2,128)S(1)} %broadcast.138), channel_id=1, source_target_pairs={{0,8},{8,16},{16,24},{1,9},{9,17},{17,25},{2,10},{10,18},{18,26},{... | collective-permute-start | bytes 3080 | tf_op jit(solution)/shard_map/ppermute | solution.py:23
  140.7 73.0 %collective-permute-start.45 = (f32[1,2,128]{2,1,0:T(2,128)S(1)}, f32[1,2,128]{2,1,0:T(2,128)S(1)}, u32[]{:S(2)}, u32[]{:S(2)}) collective-permute-start(f32[1,2,128]{2,1,0:T(2,128)S(1)} %get-tuple-element.85), channel_id=1, source_target_pairs={{0,8},{8,16},{16,24},{1,9},{9,17},{17,25},{2,10},{10,18},{18,26},{... | collective-permute-start | bytes 3080 | tf_op jit(solution)/shard_map/ppermute | solution.py:13
  151.3 6.8 %collective-permute-start.30 = (f32[6,1,256]{2,1,0:T(1,128)S(1)}, f32[6,1,256]{2,1,0:T(1,128)S(1)}, u32[]{:S(2)}, u32[]{:S(2)}) collective-permute-start(f32[6,1,256]{2,1,0:T(1,128)S(1)} %get-tuple-element.45), channel_id=1, source_target_pairs={{1,0},{2,1},{3,2},{4,3},{5,4},{6,5},{7,6},{9,8},{10,9},{11,10},{12... | collective-permute-start | bytes 18440 | tf_op jit(solution)/shard_map/ppermute | solution.py:24
  156.2 6.4 %collective-permute-start.31 = (f32[6,1,256]{2,1,0:T(1,128)S(1)}, f32[6,1,256]{2,1,0:T(1,128)S(1)}, u32[]{:S(2)}, u32[]{:S(2)}) collective-permute-start(f32[6,1,256]{2,1,0:T(1,128)S(1)} %get-tuple-element.46), channel_id=1, source_target_pairs={{0,1},{1,2},{2,3},{3,4},{4,5},{5,6},{6,7},{8,9},{9,10},{10,11},{11... | collective-permute-start | bytes 18440 | tf_op jit(solution)/shard_map/ppermute | solution.py:23
  171.5 6.4 %collective-permute-start.35 = (f32[6,1,256]{2,1,0:T(1,128)S(1)}, f32[6,1,256]{2,1,0:T(1,128)S(1)}, u32[]{:S(2)}, u32[]{:S(2)}) collective-permute-start(f32[6,1,256]{2,1,0:T(1,128)S(1)} %get-tuple-element.44), channel_id=1, source_target_pairs={{0,1},{1,2},{2,3},{3,4},{4,5},{5,6},{6,7},{8,9},{9,10},{10,11},{11... | collective-permute-start | bytes 18440 | tf_op jit(solution)/shard_map/ppermute | solution.py:23
  175.5 38.2 %collective-permute-start.48 = (f32[2,1,128]{2,1,0:T(1,128)S(1)}, f32[2,1,128]{2,1,0:T(1,128)S(1)}, u32[]{:S(2)}, u32[]{:S(2)}) collective-permute-start(f32[2,1,128]{2,1,0:T(1,128)S(1)} %get-tuple-element.87), channel_id=1, source_target_pairs={{0,1},{1,2},{2,3},{3,4},{4,5},{5,6},{6,7},{8,9},{9,10},{10,11},{11... | collective-permute-start | bytes 3080 | tf_op jit(solution)/shard_map/ppermute | solution.py:13
  200.2 13.5 %collective-permute-start.47 = (f32[4,1,128]{2,1,0:T(1,128)S(1)}, f32[4,1,128]{2,1,0:T(1,128)S(1)}, u32[]{:S(2)}, u32[]{:S(2)}) collective-permute-start(f32[4,1,128]{2,1,0:T(1,128)S(1)} %get-tuple-element.71), channel_id=1, source_target_pairs={{1,0},{2,1},{3,2},{4,3},{5,4},{6,5},{7,6},{9,8},{10,9},{11,10},{12... | collective-permute-start | bytes 6152 | tf_op jit(solution)/shard_map/ppermute | solution.py:24
  (46 other events, 436.8 us)
where the time goes:
time: 266 us; the launch traced here: 264 us
  starting transfers between devices  159 us (60%)
  waiting for transfers between devices  55.4 us (21%)
  local copies, waits for them, and re-layouts  31.9 us (12%)
  other arithmetic  15 us (6%)
    ppermute x28, starting transfers between devices, padded_2(): after = lax.ppermute(first, axis, down)  77.5 us
    ppermute x28, starting transfers between devices, padded_2(): before = lax.ppermute(last, axis, up)  68.9 us
    ppermute x28, waiting for transfers between devices, padded_2(): before = lax.ppermute(last, axis, up)  55.3 us
    reshape x3, local copies, waits for them, and re-layouts, coarsen_cells(): field.reshape(nx // 2, 2, ny // 2, 2, nz // 2, 2).mean(axis=(1, 3, 5))  20.5 us
    ppermute x6, starting transfers between devices, from_behind(): return lax.ppermute(block, axis, route)  13 us
    reduce_sum x4, other arithmetic, coarsen_cells(): field.reshape(nx // 2, 2, ny // 2, 2, nz // 2, 2).mean(axis=(1, 3, 5))  8.36 us
  transfers between devices with their start and end apart: 62, of which 22 were waited for; matrix products, arithmetic and copies ran while one was open for 17% of the time, Pallas kernels for 0%

commit v1 on v0

v1 whole, which is shorter than its diff:
```python
import functools

import jax
import jax.numpy as jnp
from jax import lax
from jax.experimental import pallas as pl
from jax.experimental.pallas import tpu as pltpu
from jax.sharding import PartitionSpec as P

LEVELS = 3
ROW = 8

FACES = ((1, 0), (-1, 0), (0, 1), (0, -1))
CORNERS = ((1, 1), (1, -1), (-1, 1), (-1, -1))
AROUND = FACES + CORNERS


def layer_shape(dims, way):
    nx, ny, nz = dims
    return (1 if way[0] else nx, 1 if way[1] else ny, nz)


def edge_shape(dims, way):
    return (2, 1, 1, dims[2])


def messages(dims_of):
    found = {}
    for way in FACES:
        found[("first", 0, way)] = layer_shape(dims_of[0], way)
    for level, dims in enumerate(dims_of):
        for way in ((1, 0), (0, 1)):
            found[("lower", level, way)] = layer_shape(dims, way)
        for way in FACES:
            found[("toward", level, way)] = layer_shape(dims, way)
            found[("ends", level, way)] = edge_shape(dims, way)
        for half in range(2):
            ways = FACES if (level == LEVELS - 1 and half == 1) else AROUND
            for way in ways:
                found[("half%d" % half, level, way)] = layer_shape(dims, way)
    return found


def at_side(dims, way):
    nx, ny, _ = dims
    xs = {0: slice(0, nx), 1: slice(nx - 1, nx), -1: slice(0, 1)}[way[0]]
    ys = {0: slice(0, ny), 1: slice(ny - 1, ny), -1: slice(0, 1)}[way[1]]
    return xs, ys


def halo_place(dims, way):
    nx, ny, _ = dims
    xs = {0: slice(1, 1 + nx), 1: slice(nx + 1, nx + 2), -1: slice(0, 1)}[way[0]]
    ys = {0: slice(ROW, ROW + ny), 1: slice(ROW + ny, ROW + ny + 1), -1: slice(ROW - 1, ROW)}[way[1]]
    return xs, ys


def parity_at(shape, offset=0):
    total = (
        lax.broadcasted_iota(jnp.int32, shape, 0)
        + lax.broadcasted_iota(jnp.int32, shape, 1)
        + lax.broadcasted_iota(jnp.int32, shape, 2)
        + offset
    )
    return (total & 1) == 1


def kernel(dims_of, keys, *refs):
    refs = list(refs)
    u_in, f_in, a_in, bx_in, by_in, bz_in = refs[:6]
    outs = refs[6:9]
    refs = refs[9:]
    n_keys = len(keys)
    out_buf = dict(zip(keys, refs[:n_keys]))
    in_buf = dict(zip(keys, refs[n_keys : 2 * n_keys]))
    refs = refs[2 * n_keys :]
    names = ("open", "shut", "g", "diag", "xu", "xl", "yu", "yl", "zu", "zl", "a", "bx", "by", "bz")
    per = []
    for level in range(LEVELS):
        per.append(dict(zip(names, refs[: len(names)])))
        refs = refs[len(names) :]
    pair_t, cols_t = refs[0:2], refs[2:4]
    send_sem, recv_sem = refs[4], refs[5]

    gx, gy = lax.axis_index("gx"), lax.axis_index("gy")
    n_x, n_y = lax.axis_size("gx"), lax.axis_size("gy")

    def inside(dx, dy):
        ok = None
        for place, step, count in ((gx, dx, n_x), (gy, dy, n_y)):
            if step == 0:
                continue
            here = (place + step < count) if step > 0 else (place + step >= 0)
            ok = here if ok is None else jnp.logical_and(ok, here)
        return ok

    def copy_of(key):
        way = key[2]
        index = keys.index(key)
        return pltpu.make_async_remote_copy(
            src_ref=out_buf[key],
            dst_ref=in_buf[key],
            send_sem=send_sem.at[index],
            recv_sem=recv_sem.at[index],
            device_id={"gx": gx + way[0], "gy": gy + way[1]},
            device_id_type=pl.DeviceIdType.MESH,
        )

    def send(group):
        for way in AROUND:
            chosen = [key for key in group if key[2] == way]
            if chosen:

                @pl.when(inside(*way))
                def _():
                    for key in chosen:
                        copy_of(key).start()

    def receive(group):
        for way in AROUND:
            chosen = [key for key in group if key[2] == way]
            if chosen:

                @pl.when(inside(-way[0], -way[1]))
                def _():
                    for key in chosen:
                        copy_of(key).wait_recv()

    def group_of(kind, level):
        return [key for key in keys if key[0] == kind and key[1] == level]

    barrier = pltpu.get_barrier_semaphore()
    for way in AROUND:

        @pl.when(inside(*way))
        def _():
            pl.semaphore_signal(
                barrier,
                inc=1,
                device_id={"gx": gx + way[0], "gy": gy + way[1]},
                device_id_type=pl.DeviceIdType.MESH,
            )

    per[0]["a"][...] = a_in[...].astype(jnp.float32)
    per[0]["bx"][...] = bx_in[...].astype(jnp.float32)
    per[0]["by"][...] = by_in[...].astype(jnp.float32)
    per[0]["bz"][...] = bz_in[...].astype(jnp.float32)

    def put_faces(kind, level, source, ways):
        for way in ways:
            xs, ys = at_side(dims_of[level], way)
            out_buf[(kind, level, way)][...] = source[xs, ys, :]

    put_faces("first", 0, u_in, FACES)

    def put_lower(level):
        for way, name in (((1, 0), "bx"), ((0, 1), "by")):
            xs, ys = at_side(dims_of[level], way)
            out_buf[("lower", level, way)][...] = per[level][name][xs, ys, :]

    put_lower(0)

    for way in AROUND:
        chosen = [key for key in keys if key[2] == way]

        @pl.when(jnp.logical_not(inside(-way[0], -way[1])))
        def _():
            for key in chosen:
                in_buf[key][...] = jnp.zeros(in_buf[key].shape, jnp.float32)

    beside_x = (gx > 0).astype(jnp.int32) + (gx + 1 < n_x).astype(jnp.int32)
    beside_y = (gy > 0).astype(jnp.int32) + (gy + 1 < n_y).astype(jnp.int32)
    pl.semaphore_wait(barrier, beside_x + beside_y + beside_x * beside_y)

    send(group_of("first", 0) + group_of("lower", 0))

    def pair_matrix(size):
        fine = lax.broadcasted_iota(jnp.int32, (size, size // 2), 0)
        coarse = lax.broadcasted_iota(jnp.int32, (size, size // 2), 1)
        return jnp.where((fine >> 1) == coarse, 1.0, 0.0).astype(jnp.bfloat16)

    def three(v):
        high = v.astype(jnp.bfloat16)
        rest = v - high.astype(jnp.float32)
        mid = rest.astype(jnp.bfloat16)
        low = (rest - mid.astype(jnp.float32)).astype(jnp.bfloat16)
        return [high, mid, low]

    def sum_pairs_z(v):
        rows, size = v.shape
        parts = jnp.concatenate(three(v), axis=0)
        got = jnp.dot(parts, pair_matrix(size), preferred_element_type=jnp.float32)
        return got[:rows] + got[rows : 2 * rows] + got[2 * rows :]

    def squeeze(level, sources, ways):
        nx, ny, nz = dims_of[level]
        tmp, cols = pair_t[level], cols_t[level]
        hx, hy = nx // 2, ny // 2
        kept = len(sources)
        odd = (lax.broadcasted_iota(jnp.int32, (1, 1, nz), 2) & 1) == 1
        for n, (source, way) in enumerate(zip(sources, ways)):
            for i in range(hx):
                v = source(2 * i + 1)
                if way != 0:
                    v = source(2 * i) + v
                tmp[n * hx + i : n * hx + i + 1] = v
            some = slice(n * hx, (n + 1) * hx)
            for j in range(hy):
                v = tmp[some, 2 * j + 1 : 2 * j + 2, :]
                if way != 1:
                    v = v + tmp[some, 2 * j : 2 * j + 1, :]
                if way == 2:
                    v = jnp.where(odd, v, 0.0)
                cols[some, j : j + 1, :] = v * (0.125 if way is None else 0.25)
        total = kept * hx
        flat = cols[0:total].reshape(total * 8, nz)
        got = sum_pairs_z(flat).reshape(total, 8, nz // 2)
        return [got[n * hx : (n + 1) * hx, 0:hy, :] for n in range(kept)]

    def coarse_coefs(level):
        these = per[level]
        names = ("a", "bx", "by", "bz")
        sources = [
            functools.partial(lambda ref, i: ref[i : i + 1], these[name]) for name in names
        ]
        for name, v in zip(names, squeeze(level, sources, (None, 0, 1, 2))):
            per[level + 1][name][...] = v

    for level in range(1, LEVELS):
        coarse_coefs(level - 1)
        put_lower(level)
        send(group_of("lower", level))

    def make_coefs(level):
        these = per[level]
        nx, ny, nz = dims_of[level]
        scale = 0.25**level
        lower_x = in_buf[("lower", level, (1, 0))]
        lower_y = in_buf[("lower", level, (0, 1))]
        pad = these["open"]
        last = lax.broadcasted_iota(jnp.int32, (nx, ny, nz), 2)
        bx, by, bz = these["bx"][...], these["by"][...], these["bz"][...]
        bxl = jnp.concatenate([lower_x[...], bx[:-1]], axis=0) if nx > 1 else lower_x[...]
        pad[1 : 1 + nx, ROW : ROW + ny, :] = by
        pad[1 : 1 + nx, ROW - 1 : ROW, :] = lower_y[...]
        byl = pad[1 : 1 + nx, ROW - 1 : ROW - 1 + ny, :]
        bzl = jnp.where(last == 0, 0.0, pltpu.roll(bz, 1, 2))
        diag = these["a"][...] + scale * ((bx + bxl) + (by + byl) + (bz + bzl))
        over = 1.0 / diag
        these["diag"][...] = diag
        over_s = over * scale
        these["xu"][...] = bx * over_s
        these["xl"][...] = bxl * over_s
        these["yu"][...] = by * over_s
        these["yl"][...] = byl * over_s
        these["zu"][...] = jnp.where(last == nz - 1, 0.0, bz * over_s)
        these["zl"][...] = bzl * over_s
        return over

    toward_name = {(1, 0): "xu", (-1, 0): "xl", (0, 1): "yu", (0, -1): "yl"}

    def end_ways(way):
        return ((way[0], -1), (way[0], 1)) if way[0] else ((-1, way[1]), (1, way[1]))

    def cross(way, corner):
        return (0, corner[1]) if way[0] else (corner[0], 0)

    def put_toward(level):
        these = per[level]
        dims = dims_of[level]
        nx, ny, nz = dims
        for way in FACES:
            xs, ys = at_side(dims, way)
            shape = layer_shape(dims, way)
            offset = (xs.start + ys.start) & 1
            out_buf[("toward", level, way)][...] = jnp.where(
                parity_at(shape, offset), these[toward_name[way]][xs, ys, :], 0.0
            )
            for n, corner in enumerate(end_ways(way)):
                cxs, cys = at_side(dims, corner)
                offset = (cxs.start + cys.start) & 1
                out_buf[("ends", level, way)][n] = jnp.where(
                    parity_at((1, 1, nz), offset),
                    these[toward_name[cross(way, corner)]][cxs, cys, :],
                    0.0,
                )
        send(group_of("toward", level) + group_of("ends", level))

    def sums(level, pad):
        these = per[level]
        nx, ny, nz = dims_of[level]
        own = pad[1 : 1 + nx, ROW : ROW + ny, :]
        total = these["g"][...]
        total = total + these["xu"][...] * pad[2 : 2 + nx, ROW : ROW + ny, :]
        total = total + these["xl"][...] * pad[0:nx, ROW : ROW + ny, :]
        total = total + these["yu"][...] * pad[1 : 1 + nx, ROW + 1 : ROW + 1 + ny, :]
        total = total + these["yl"][...] * pad[1 : 1 + nx, ROW - 1 : ROW - 1 + ny, :]
        total = total + these["zu"][...] * pltpu.roll(own, nz - 1, 2)
        total = total + these["zl"][...] * pltpu.roll(own, 1, 2)
        return own, total

    def half_sweep(level, half, red):
        these = per[level]
        dims = dims_of[level]
        nx, ny, nz = dims
        shut, pad = these["shut"], these["open"]
        kind = "half%d" % half
        black = parity_at(dims)
        shut[1 : 1 + nx, ROW : ROW + ny, :] = red
        _, total = sums(level, shut)
        value = jnp.where(black, total, red)
        pad[1 : 1 + nx, ROW : ROW + ny, :] = value
        group = group_of(kind, level)
        for key in group:
            xs, ys = at_side(dims, key[2])
            out_buf[key][...] = pad[
                xs.start + 1 : xs.stop + 1, ys.start + ROW : ys.stop + ROW, :
            ]
        send(group)

    def finish_half(level, half, last):
        these = per[level]
        dims = dims_of[level]
        nx, ny, nz = dims
        pad = these["open"]
        kind = "half%d" % half
        group = group_of(kind, level)
        receive(group)
        if half == 0:
            receive(group_of("toward", level) + group_of("ends", level))
        back = lambda way: (-way[0], -way[1])
        if not last:
            for way in FACES:
                xs, ys = at_side(dims, way)
                mine = out_buf[(kind, level, way)][...]
                theirs = in_buf[(kind, level, back(way))][...]
                theirs = theirs + in_buf[("toward", level, back(way))][...] * mine
                hx, hy = halo_place(dims, way)
                pad[hx, hy, :] = theirs
                ends = in_buf[("ends", level, back(way))]
                for n, corner in enumerate(end_ways(way)):
                    cx, cy = at_side(dims, corner)
                    px = hx if way[0] else slice(1 + cx.start, 1 + cx.stop)
                    py = hy if way[1] else slice(ROW + cy.start, ROW + cy.stop)
                    column = in_buf[(kind, level, back(corner))][...]
                    pad[px, py, :] = pad[px, py, :] + ends[n] * column
        for way in FACES:
            xs, ys = at_side(dims, way)
            px = slice(1 + xs.start, 1 + xs.stop)
            py = slice(ROW + ys.start, ROW + ys.stop)
            theirs = in_buf[(kind, level, back(way))][...]
            pad[px, py, :] = pad[px, py, :] + out_buf[("toward", level, way)][...] * theirs

    for level in range(LEVELS):
        these = per[level]
        nx, ny, nz = dims_of[level]
        these["shut"][...] = jnp.zeros(these["shut"].shape, jnp.float32)

    source = None
    for level in range(LEVELS):
        these = per[level]
        dims = dims_of[level]
        nx, ny, nz = dims
        pad = these["open"]
        red_cells = jnp.logical_not(parity_at(dims))
        if level == 0:
            receive(group_of("lower", 0))
            these["g"][...] = f_in[...] * make_coefs(0)
            receive(group_of("first", 0))
            pad[1 : 1 + nx, ROW : ROW + ny, :] = u_in[...]
            for way in FACES:
                hx, hy = halo_place(dims, way)
                pad[hx, hy, :] = in_buf[("first", 0, (-way[0], -way[1]))][...]
            own, total = sums(0, pad)
            half_sweep(0, 0, jnp.where(red_cells, total, own))
            put_toward(0)
            for other in range(1, LEVELS):
                receive(group_of("lower", other))
                per[other]["g"][...] = make_coefs(other)
                put_toward(other)
        else:
            these["g"][...] = source * these["g"][...]
            half_sweep(level, 0, jnp.where(red_cells, these["g"][...], 0.0))
        finish_half(level, 0, False)
        own, total = sums(level, pad)
        half_sweep(level, 1, jnp.where(red_cells, total, own))
        finish_half(level, 1, level == LEVELS - 1)
        outs[level][...] = pad[1 : 1 + nx, ROW : ROW + ny, :]
        if level + 1 < LEVELS:
            own, total = sums(level, pad)
            these["a"][...] = jnp.where(red_cells, these["diag"][...] * (total - own), 0.0)
            take = functools.partial(lambda ref, i: ref[i : i + 1], these["a"])
            source = squeeze(level, [take], (None,))[0]

    for way in AROUND:
        chosen = [key for key in keys if key[2] == way]

        @pl.when(inside(*way))
        def _():
            for key in chosen:
                copy_of(key).wait_send()


def shards(solution, right_side, alpha, beta_x, beta_y, beta_z):
    dims_of = [tuple(size >> level for size in solution.shape) for level in range(LEVELS)]
    found = messages(dims_of)
    keys = list(found)
    buffers = [pltpu.VMEM(found[key], jnp.float32) for key in keys]
    scratch = buffers + buffers
    for nx, ny, nz in dims_of:
        rows = 24 if ny + 1 > 8 else 16
        scratch += [pltpu.VMEM((nx + 2, rows, nz), jnp.float32)] * 2
        scratch += [pltpu.VMEM((nx, ny, nz), jnp.float32)] * 12
    for nx, ny, nz in dims_of[:2]:
        scratch += [pltpu.VMEM((4 * nx // 2, ny, nz), jnp.float32)]
    for nx, ny, nz in dims_of[:2]:
        scratch += [pltpu.VMEM((4 * nx // 2, 8, nz), jnp.float32)]
    scratch += [pltpu.SemaphoreType.DMA((len(keys),))] * 2
    return pl.pallas_call(
        functools.partial(kernel, dims_of, keys),
        out_shape=[jax.ShapeDtypeStruct(dims, jnp.float32) for dims in dims_of],
        in_specs=[pl.BlockSpec(memory_space=pltpu.VMEM)] * 6,
        out_specs=[pl.BlockSpec(memory_space=pltpu.VMEM)] * 3,
        scratch_shapes=scratch,
        compiler_params=pltpu.CompilerParams(
            collective_id=0, has_side_effects=True, vmem_limit_bytes=48 * 1024 * 1024
        ),
        name="vcycle",
    )(solution, right_side, alpha, beta_x, beta_y, beta_z)


def solution(mesh):
    place = P("gx", "gy", None)
    return jax.shard_map(
        shards,
        mesh=mesh,
        in_specs=(place,) * 6,
        out_specs=(place,) * 3,
        check_vma=False,
    )
```

time: 266 us -> 37.7 us (0.14)
  the two profiles are of different devices: /device:TPU:26 before, /device:TPU:0 now
where the time goes in v1:
time: 37.7 us; the launch traced here: 37.3 us
  Pallas kernels  29.7 us (79%)
  local copies, waits for them, and re-layouts  7 us (19%)
  between operations  0.65 us (2%)
    pallas_call x1, Pallas kernels, shards(): pl.pallas_call(functools.partial(kernel, dims_of, keys), out_shape=[jax.S...  29.7 us
    unnamed x15, local copies, waits for them, and re-layouts  7 us

profile of v1, /device:TPU:0, one launch (start us, length us, event | category | flops | bytes accessed | tf_op | source)
XLA Modules:
  0.0 37.3 jit_solution(13668064973414141284)
XLA Ops:
  0.6 0.0 copy-start
  0.6 0.9 %copy-done = f32[8,8,512]{2,1,0:T(8,128)S(1)} copy-done((f32[8,8,512]{2,1,0:T(8,128)S(1)}, f32[8,8,512]{2,1,0:T(8,128)}, u32[]{:S(2)}) %copy-start) | copy-done | bytes 131096
  1.5 0.0 copy-start.1
  1.5 0.9 %copy-done.1 = f32[8,8,512]{2,1,0:T(8,128)S(1)} copy-done((f32[8,8,512]{2,1,0:T(8,128)S(1)}, f32[8,8,512]{2,1,0:T(8,128)}, u32[]{:S(2)}) %copy-start.1) | copy-done | bytes 131096
  2.4 0.0 copy-start.2
  2.4 0.8 %copy-done.2 = bf16[8,8,512]{2,1,0:T(8,128)(2,1)S(1)} copy-done((bf16[8,8,512]{2,1,0:T(8,128)(2,1)S(1)}, bf16[8,8,512]{2,1,0:T(8,128)(2,1)}, u32[]{:S(2)}) %copy-start.2) | copy-done | bytes 65560
  3.3 0.0 copy-start.3
  3.3 0.8 %copy-done.3 = bf16[8,8,512]{2,1,0:T(8,128)(2,1)S(1)} copy-done((bf16[8,8,512]{2,1,0:T(8,128)(2,1)S(1)}, bf16[8,8,512]{2,1,0:T(8,128)(2,1)}, u32[]{:S(2)}) %copy-start.3) | copy-done | bytes 65560
  4.1 0.0 copy-start.4
  4.1 0.8 %copy-done.4 = bf16[8,8,512]{2,1,0:T(8,128)(2,1)S(1)} copy-done((bf16[8,8,512]{2,1,0:T(8,128)(2,1)S(1)}, bf16[8,8,512]{2,1,0:T(8,128)(2,1)}, u32[]{:S(2)}) %copy-start.4) | copy-done | bytes 65560
  5.0 0.0 copy-start.5
  5.0 0.8 %copy-done.5 = bf16[8,8,512]{2,1,0:T(8,128)(2,1)S(1)} copy-done((bf16[8,8,512]{2,1,0:T(8,128)(2,1)S(1)}, bf16[8,8,512]{2,1,0:T(8,128)(2,1)}, u32[]{:S(2)}) %copy-start.5) | copy-done | bytes 65560
  5.8 29.7 %vcycle.1 = (f32[8,8,512]{2,1,0:T(8,128)S(1)}, f32[4,4,256]{2,1,0:T(4,128)S(1)}, f32[2,2,128]{2,1,0:T(2,128)S(1)}) custom-call(f32[8,8,512]{2,1,0:T(8,128)S(1)} %copy-done, f32[8,8,512]{2,1,0:T(8,128)S(1)} %copy-done.1, bf16[8,8,512]{2,1,0:T(8,128)(2,1)S(1)} %copy-done.2, bf16[8,8,512]{2,1,0:T(8,128)(2,1)S(1)} %copy-done.3, ...), custom_call_target="tpu_custom_call" | custom-call | tf_op jit(solution)/shard_map/vcycle/pallas_call | solution.py:419
  35.5 0.7 %copy.12 = f32[8,8,512]{2,1,0:T(8,128)} copy(f32[8,8,512]{2,1,0:T(8,128)S(1)} %get-tuple-element.6) | data formatting | bytes 262144
  36.2 0.6 %copy.13 = f32[4,4,256]{2,1,0:T(4,128)} copy(f32[4,4,256]{2,1,0:T(4,128)S(1)} %get-tuple-element.7) | data formatting | bytes 32768
  36.8 0.6 %copy.14 = f32[2,2,128]{2,1,0:T(2,128)} copy(f32[2,2,128]{2,1,0:T(2,128)S(1)} %get-tuple-element.8) | data formatting | bytes 4096
Async XLA Ops:
  0.6 0.9 %copy-start = (f32[8,8,512]{2,1,0:T(8,128)S(1)}, f32[8,8,512]{2,1,0:T(8,128)}, u32[]{:S(2)}) copy-start(f32[8,8,512]{2,1,0:T(8,128)} %refs_0_.1) | copy-start | bytes 393220
  1.5 0.9 %copy-start.1 = (f32[8,8,512]{2,1,0:T(8,128)S(1)}, f32[8,8,512]{2,1,0:T(8,128)}, u32[]{:S(2)}) copy-start(f32[8,8,512]{2,1,0:T(8,128)} %refs_1_.1) | copy-start | bytes 393220
  2.4 0.8 %copy-start.2 = (bf16[8,8,512]{2,1,0:T(8,128)(2,1)S(1)}, bf16[8,8,512]{2,1,0:T(8,128)(2,1)}, u32[]{:S(2)}) copy-start(bf16[8,8,512]{2,1,0:T(8,128)(2,1)} %refs_2_.1) | copy-start | bytes 196612
  3.3 0.8 %copy-start.3 = (bf16[8,8,512]{2,1,0:T(8,128)(2,1)S(1)}, bf16[8,8,512]{2,1,0:T(8,128)(2,1)}, u32[]{:S(2)}) copy-start(bf16[8,8,512]{2,1,0:T(8,128)(2,1)} %refs_3_.1) | copy-start | bytes 196612
  4.1 0.8 %copy-start.4 = (bf16[8,8,512]{2,1,0:T(8,128)(2,1)S(1)}, bf16[8,8,512]{2,1,0:T(8,128)(2,1)}, u32[]{:S(2)}) copy-start(bf16[8,8,512]{2,1,0:T(8,128)(2,1)} %refs_4_.1) | copy-start | bytes 196612
  5.0 0.8 %copy-start.5 = (bf16[8,8,512]{2,1,0:T(8,128)(2,1)S(1)}, bf16[8,8,512]{2,1,0:T(8,128)(2,1)}, u32[]{:S(2)}) copy-start(bf16[8,8,512]{2,1,0:T(8,128)(2,1)} %refs_5_.1) | copy-start | bytes 196612

commit v2 on v1

--- a/solution.py
+++ b/solution.py
@@ -8,6 +8,7 @@
 from jax.sharding import PartitionSpec as P
 
 LEVELS = 3
+VMEM_LIMIT = (64 * 1024 - 160) * 1024
 ROW = 8
 
 FACES = ((1, 0), (-1, 0), (0, 1), (0, -1))
@@ -67,9 +68,12 @@
 
 def kernel(dims_of, keys, *refs):
     refs = list(refs)
-    u_in, f_in, a_in, bx_in, by_in, bz_in = refs[:6]
+    args = refs[:6]
     outs = refs[6:9]
-    refs = refs[9:]
+    u_in, f_in, a_in, bx_in, by_in, bz_in = held = refs[9:15]
+    load_sem, store_sem = refs[15:17]
+    kept = refs[17:20]
+    refs = refs[20:]
     n_keys = len(keys)
     out_buf = dict(zip(keys, refs[:n_keys]))
     in_buf = dict(zip(keys, refs[n_keys : 2 * n_keys]))
@@ -129,6 +133,9 @@
     def group_of(kind, level):
         return [key for key in keys if key[0] == kind and key[1] == level]
 
+    stores = [pltpu.make_async_copy(kept[n], outs[n], store_sem.at[n]) for n in range(LEVELS)]
+    loads = [pltpu.make_async_copy(args[n], held[n], load_sem.at[n]) for n in range(6)]
+
     barrier = pltpu.get_barrier_semaphore()
     for way in AROUND:
 
@@ -141,16 +148,15 @@
                 device_id_type=pl.DeviceIdType.MESH,
             )
 
-    per[0]["a"][...] = a_in[...].astype(jnp.float32)
-    per[0]["bx"][...] = bx_in[...].astype(jnp.float32)
-    per[0]["by"][...] = by_in[...].astype(jnp.float32)
-    per[0]["bz"][...] = bz_in[...].astype(jnp.float32)
+    for n in (0, 3, 4, 2, 5, 1):
+        loads[n].start()
 
     def put_faces(kind, level, source, ways):
         for way in ways:
             xs, ys = at_side(dims_of[level], way)
             out_buf[(kind, level, way)][...] = source[xs, ys, :]
 
+    loads[0].wait()
     put_faces("first", 0, u_in, FACES)
 
     def put_lower(level):
@@ -158,6 +164,10 @@
             xs, ys = at_side(dims_of[level], way)
             out_buf[("lower", level, way)][...] = per[level][name][xs, ys, :]
 
+    loads[3].wait()
+    per[0]["bx"][...] = bx_in[...].astype(jnp.float32)
+    loads[4].wait()
+    per[0]["by"][...] = by_in[...].astype(jnp.float32)
     put_lower(0)
 
     for way in AROUND:
@@ -173,6 +183,11 @@
     pl.semaphore_wait(barrier, beside_x + beside_y + beside_x * beside_y)
 
     send(group_of("first", 0) + group_of("lower", 0))
+    loads[2].wait()
+    per[0]["a"][...] = a_in[...].astype(jnp.float32)
+    loads[5].wait()
+    per[0]["bz"][...] = bz_in[...].astype(jnp.float32)
+    loads[1].wait()
 
     def pair_matrix(size):
         fine = lax.broadcasted_iota(jnp.int32, (size, size // 2), 0)
@@ -385,7 +400,8 @@
         own, total = sums(level, pad)
         half_sweep(level, 1, jnp.where(red_cells, total, own))
         finish_half(level, 1, level == LEVELS - 1)
-        outs[level][...] = pad[1 : 1 + nx, ROW : ROW + ny, :]
+        kept[level][...] = pad[1 : 1 + nx, ROW : ROW + ny, :]
+        stores[level].start()
         if level + 1 < LEVELS:
             own, total = sums(level, pad)
             these["a"][...] = jnp.where(red_cells, these["diag"][...] * (total - own), 0.0)
@@ -400,13 +416,29 @@
             for key in chosen:
                 copy_of(key).wait_send()
 
+    for copy in stores:
+        copy.wait()
+
+
+def store(fine, middle, coarse, fine_out, middle_out, coarse_out, sem):
+    pairs = ((fine, fine_out), (middle, middle_out), (coarse, coarse_out))
+    copies = [pltpu.make_async_copy(src, dst, sem.at[n]) for n, (src, dst) in enumerate(pairs)]
+    for copy in copies:
+        copy.start()
+    for copy in copies:
+        copy.wait()
+
 
 def shards(solution, right_side, alpha, beta_x, beta_y, beta_z):
     dims_of = [tuple(size >> level for size in solution.shape) for level in range(LEVELS)]
     found = messages(dims_of)
     keys = list(found)
     buffers = [pltpu.VMEM(found[key], jnp.float32) for key in keys]
-    scratch = buffers + buffers
+    fine = dims_of[0]
+    scratch = [pltpu.VMEM(fine, jnp.float32)] * 2 + [pltpu.VMEM(fine, jnp.bfloat16)] * 4
+    scratch += [pltpu.SemaphoreType.DMA((6,)), pltpu.SemaphoreType.DMA((LEVELS,))]
+    scratch += [pltpu.VMEM(dims, jnp.float32) for dims in dims_of]
+    scratch += buffers + buffers
     for nx, ny, nz in dims_of:
         rows = 24 if ny + 1 > 8 else 16
         scratch += [pltpu.VMEM((nx + 2, rows, nz), jnp.float32)] * 2
@@ -416,17 +448,26 @@
     for nx, ny, nz in dims_of[:2]:
         scratch += [pltpu.VMEM((4 * nx // 2, 8, nz), jnp.float32)]
     scratch += [pltpu.SemaphoreType.DMA((len(keys),))] * 2
-    return pl.pallas_call(
+    iterates = pl.pallas_call(
         functools.partial(kernel, dims_of, keys),
         out_shape=[jax.ShapeDtypeStruct(dims, jnp.float32) for dims in dims_of],
-        in_specs=[pl.BlockSpec(memory_space=pltpu.VMEM)] * 6,
-        out_specs=[pl.BlockSpec(memory_space=pltpu.VMEM)] * 3,
+        in_specs=[pl.BlockSpec(memory_space=pltpu.HBM)] * 6,
+        out_specs=[pl.BlockSpec(memory_space=pltpu.HBM)] * 3,
         scratch_shapes=scratch,
         compiler_params=pltpu.CompilerParams(
-            collective_id=0, has_side_effects=True, vmem_limit_bytes=48 * 1024 * 1024
+            collective_id=0, has_side_effects=True, vmem_limit_bytes=VMEM_LIMIT
         ),
         name="vcycle",
     )(solution, right_side, alpha, beta_x, beta_y, beta_z)
+    return pl.pallas_call(
+        store,
+        out_shape=[jax.ShapeDtypeStruct(dims, jnp.float32) for dims in dims_of],
+        in_specs=[pl.BlockSpec(memory_space=pltpu.HBM)] * 3,
+        out_specs=[pl.BlockSpec(memory_space=pltpu.HBM)] * 3,
+        scratch_shapes=[pltpu.SemaphoreType.DMA((3,))],
+        compiler_params=pltpu.CompilerParams(vmem_limit_bytes=VMEM_LIMIT),
+        name="store",
+    )(*iterates)
 
 
 def solution(mesh):

time: 37.7 us -> 36.7 us (0.973)
  local copies, waits for them, and re-layouts: 7 us -> 0 us
  Pallas kernels: 29.7 us -> 35.9 us
    unnamed x15 -> x0, local copies, waits for them, and re-layouts: 7 us -> none
    pallas_call x0 -> x1, Pallas kernels: none -> 5.66 us  [shards(): pl.pallas_call(store, out_shape=[jax.ShapeDtypeStruct(dims, jnp.float32)...]
    pallas_call x1, Pallas kernels: 29.7 us -> 30.3 us  [shards(): pl.pallas_call(functools.partial(kernel, dims_of, keys), out_shape=[jax.S...]
where the time goes in v2:
time: 36.7 us; the launch traced here: 36.6 us
  Pallas kernels  35.9 us (98%)
  between operations  0.64 us (2%)
    pallas_call x1, Pallas kernels, shards(): pl.pallas_call(functools.partial(kernel, dims_of, keys), out_shape=[jax.S...  30.3 us
    pallas_call x1, Pallas kernels, shards(): pl.pallas_call(store, out_shape=[jax.ShapeDtypeStruct(dims, jnp.float32)...  5.66 us

profile of v2, /device:TPU:0, one launch (start us, length us, event | category | flops | bytes accessed | tf_op | source)
XLA Modules:
  0.0 36.6 jit_solution(10470196106289380668)
XLA Ops:
  0.6 30.3 %vcycle.1 = (f32[8,8,512]{2,1,0:T(8,128)}, f32[4,4,256]{2,1,0:T(4,128)}, f32[2,2,128]{2,1,0:T(2,128)}) custom-call(f32[8,8,512]{2,1,0:T(8,128)} %refs_0_.1, f32[8,8,512]{2,1,0:T(8,128)} %refs_1_.1, bf16[8,8,512]{2,1,0:T(8,128)(2,1)} %refs_2_.1, bf16[8,8,512]{2,1,0:T(8,128)(2,1)} %refs_3_.1, bf16[8,8,512]{2,1,0:T(8,128)(2,1)} %refs_4_.1, ...), custom_call_target="tpu_custom_call" | custom-call | tf_op jit(solution)/shard_map/vcycle/pallas_call | solution.py:451
  30.9 5.7 %store.1 = (f32[8,8,512]{2,1,0:T(8,128)}, f32[4,4,256]{2,1,0:T(4,128)}, f32[2,2,128]{2,1,0:T(2,128)}) custom-call(f32[8,8,512]{2,1,0:T(8,128)} %get-tuple-element.6.fine, f32[4,4,256]{2,1,0:T(4,128)} %get-tuple-element.7.middle, f32[2,2,128]{2,1,0:T(2,128)} %get-tuple-element.8.coarse), custom_call_target="tpu_custom_call" | custom-call | tf_op jit(solution)/shard_map/store/pallas_call | solution.py:462

commit v3 on v2

--- a/solution.py
+++ b/solution.py
@@ -14,6 +14,7 @@
 FACES = ((1, 0), (-1, 0), (0, 1), (0, -1))
 CORNERS = ((1, 1), (1, -1), (-1, 1), (-1, -1))
 AROUND = FACES + CORNERS
+WIDE = AROUND + ((2, 0), (-2, 0), (0, 2), (0, -2))
 
 
 def layer_shape(dims, way):
@@ -29,15 +30,17 @@
     found = {}
     for way in FACES:
         found[("first", 0, way)] = layer_shape(dims_of[0], way)
-    for level, dims in enumerate(dims_of):
+    for way in WIDE:
+        found[("raw", LEVELS - 1, way)] = (16, dims_of[-1][2])
+        found[("source", LEVELS - 1, way)] = (8, dims_of[-1][2])
+    for level, dims in enumerate(dims_of[:-1]):
         for way in ((1, 0), (0, 1)):
             found[("lower", level, way)] = layer_shape(dims, way)
         for way in FACES:
             found[("toward", level, way)] = layer_shape(dims, way)
             found[("ends", level, way)] = edge_shape(dims, way)
         for half in range(2):
-            ways = FACES if (level == LEVELS - 1 and half == 1) else AROUND
-            for way in ways:
+            for way in AROUND:
                 found[("half%d" % half, level, way)] = layer_shape(dims, way)
     return found
 
@@ -85,6 +88,7 @@
         refs = refs[len(names) :]
     pair_t, cols_t = refs[0:2], refs[2:4]
     send_sem, recv_sem = refs[4], refs[5]
+    wide = dict(zip(("a", "bx", "by", "bz", "g", "over", "xu", "xl", "yu", "yl", "zu", "zl"), refs[6:]))
 
     gx, gy = lax.axis_index("gx"), lax.axis_index("gy")
     n_x, n_y = lax.axis_size("gx"), lax.axis_size("gy")
@@ -101,8 +105,9 @@
     def copy_of(key):
         way = key[2]
         index = keys.index(key)
+        shared = key[0] in ("raw", "source")
         return pltpu.make_async_remote_copy(
-            src_ref=out_buf[key],
+            src_ref=out_buf[key[:2] + WIDE[:1] if shared else key],
             dst_ref=in_buf[key],
             send_sem=send_sem.at[index],
             recv_sem=recv_sem.at[index],
@@ -111,7 +116,7 @@
         )
 
     def send(group):
-        for way in AROUND:
+        for way in WIDE:
             chosen = [key for key in group if key[2] == way]
             if chosen:
 
@@ -121,7 +126,7 @@
                         copy_of(key).start()
 
     def receive(group):
-        for way in AROUND:
+        for way in WIDE:
             chosen = [key for key in group if key[2] == way]
             if chosen:
 
@@ -137,7 +142,7 @@
     loads = [pltpu.make_async_copy(args[n], held[n], load_sem.at[n]) for n in range(6)]
 
     barrier = pltpu.get_barrier_semaphore()
-    for way in AROUND:
+    for way in WIDE:
 
         @pl.when(inside(*way))
         def _():
@@ -171,7 +176,7 @@
     put_lower(0)
 
     for way in AROUND:
-        chosen = [key for key in keys if key[2] == way]
+        chosen = [key for key in keys if key[2] == way and key[0] not in ("raw", "source")]
 
         @pl.when(jnp.logical_not(inside(-way[0], -way[1])))
         def _():
@@ -180,7 +185,9 @@
 
     beside_x = (gx > 0).astype(jnp.int32) + (gx + 1 < n_x).astype(jnp.int32)
     beside_y = (gy > 0).astype(jnp.int32) + (gy + 1 < n_y).astype(jnp.int32)
-    pl.semaphore_wait(barrier, beside_x + beside_y + beside_x * beside_y)
+    far_x = (gx > 1).astype(jnp.int32) + (gx + 2 < n_x).astype(jnp.int32)
+    far_y = (gy > 1).astype(jnp.int32) + (gy + 2 < n_y).astype(jnp.int32)
+    pl.semaphore_wait(barrier, beside_x + beside_y + beside_x * beside_y + far_x + far_y)
 
     send(group_of("first", 0) + group_of("lower", 0))
     loads[2].wait()
@@ -241,10 +248,12 @@
         for name, v in zip(names, squeeze(level, sources, (None, 0, 1, 2))):
             per[level + 1][name][...] = v
 
-    for level in range(1, LEVELS):
-        coarse_coefs(level - 1)
-        put_lower(level)
-        send(group_of("lower", level))
+    def prepare_coarse():
+        coarse_coefs(0)
+        put_lower(1)
+        send(group_of("lower", 1))
+        coarse_coefs(1)
+        put_raw()
 
     def make_coefs(level):
         these = per[level]
@@ -366,13 +375,89 @@
             theirs = in_buf[(kind, level, back(way))][...]
             pad[px, py, :] = pad[px, py, :] + out_buf[("toward", level, way)][...] * theirs
 
-    for level in range(LEVELS):
-        these = per[level]
-        nx, ny, nz = dims_of[level]
-        these["shut"][...] = jnp.zeros(these["shut"].shape, jnp.float32)
+    last = LEVELS - 1
+    wide_names = ("a", "bx", "by", "bz")
+
+    def put_raw():
+        buffer = out_buf[("raw", last, WIDE[0])]
+        for c, name in enumerate(wide_names):
+            for x in range(2):
+                buffer[4 * c + 2 * x : 4 * c + 2 * x + 2, :] = per[last][name][x]
+        send(group_of("raw", last))
+
+    def spread(kind, targets):
+        for way in WIDE:
+            key = (kind, last, way)
+            at = (-2 * way[0], -2 * way[1])
+
+            @pl.when(inside(-way[0], -way[1]))
+            def _():
+                copy_of(key).wait_recv()
+                for c, target in enumerate(targets):
+                    for x in range(2):
+                        if not -3 <= at[0] + x <= 4:
+                            continue
+                        ys = [y for y in range(2) if -3 <= at[1] + y <= 4]
+                        row = 4 * c + 2 * x + ys[0]
+                        to = (at[1] + ys[0]) % 8
+                        target[at[0] + x + 3, to : to + len(ys), :] = in_buf[key][
+                            row : row + len(ys), :
+                        ]
+
+    def lower_x(v):
+        return jnp.concatenate([jnp.zeros_like(v[:1]), v[:-1]], axis=0)
+
+    def upper_x(v):
+        return jnp.concatenate([v[1:], jnp.zeros_like(v[:1])], axis=0)
+
+    def wide_coefs():
+        scale = 0.25**last
+        nz = dims_of[last][2]
+        for name in wide_names:
+            wide[name][...] = jnp.zeros(wide[name].shape, jnp.float32)
+            wide[name][3:5, 0:2, :] = per[last][name][...]
+        wide["g"][...] = jnp.zeros(wide["g"].shape, jnp.float32)
+        spread("raw", [wide[name] for name in wide_names])
+        a, bx, by, bz = (wide[name][...] for name in wide_names)
+        place = lax.broadcasted_iota(jnp.int32, a.shape, 2)
+        bxl, byl = lower_x(bx), pltpu.roll(by, 1, 1)
+        bzl = jnp.where(place == 0, 0.0, pltpu.roll(bz, 1, 2))
+        diag = a + scale * ((bx + bxl) + (by + byl) + (bz + bzl))
+        over = jnp.where(a > 0.0, 1.0 / jnp.where(a > 0.0, diag, 1.0), 0.0)
+        wide["over"][...] = over
+        over = over * scale
+        wide["xu"][...], wide["xl"][...] = bx * over, bxl * over
+        wide["yu"][...], wide["yl"][...] = by * over, byl * over
+        wide["zu"][...] = jnp.where(place == nz - 1, 0.0, bz * over)
+        wide["zl"][...] = bzl * over
+
+    def wide_level(source):
+        nz = dims_of[last][2]
+        own = source * wide["over"][3:5, 0:2, :]
+        buffer = out_buf[("source", last, WIDE[0])]
+        for x in range(2):
+            buffer[2 * x : 2 * x + 2, :] = own[x]
+        send(group_of("source", last))
+        wide["g"][3:5, 0:2, :] = own
+        spread("source", [wide["g"]])
+        g = wide["g"][...]
+        black = parity_at(g.shape, 1)
+        u = jnp.where(black, 0.0, g)
+        for step in range(3):
+            total = g + wide["xu"][...] * upper_x(u) + wide["xl"][...] * lower_x(u)
+            total = total + wide["yu"][...] * pltpu.roll(u, 7, 1)
+            total = total + wide["yl"][...] * pltpu.roll(u, 1, 1)
+            total = total + wide["zu"][...] * pltpu.roll(u, nz - 1, 2)
+            total = total + wide["zl"][...] * pltpu.roll(u, 1, 2)
+            u = jnp.where(black, u, total) if step == 1 else jnp.where(black, total, u)
+        kept[last][...] = u[3:5, 0:2, :]
+        stores[last].start()
+
+    for level in range(last):
+        per[level]["shut"][...] = jnp.zeros(per[level]["shut"].shape, jnp.float32)
 
     source = None
-    for level in range(LEVELS):
+    for level in range(last):
         these = per[level]
         dims = dims_of[level]
         nx, ny, nz = dims
@@ -389,26 +474,28 @@
             own, total = sums(0, pad)
             half_sweep(0, 0, jnp.where(red_cells, total, own))
             put_toward(0)
-            for other in range(1, LEVELS):
-                receive(group_of("lower", other))
-                per[other]["g"][...] = make_coefs(other)
-                put_toward(other)
+            prepare_coarse()
         else:
             these["g"][...] = source * these["g"][...]
             half_sweep(level, 0, jnp.where(red_cells, these["g"][...], 0.0))
+            wide_coefs()
         finish_half(level, 0, False)
         own, total = sums(level, pad)
         half_sweep(level, 1, jnp.where(red_cells, total, own))
-        finish_half(level, 1, level == LEVELS - 1)
+        if level == 0:
+            receive(group_of("lower", 1))
+            per[1]["g"][...] = make_coefs(1)
+            put_toward(1)
+        finish_half(level, 1, False)
         kept[level][...] = pad[1 : 1 + nx, ROW : ROW + ny, :]
         stores[level].start()
-        if level + 1 < LEVELS:
-            own, total = sums(level, pad)
-            these["a"][...] = jnp.where(red_cells, these["diag"][...] * (total - own), 0.0)
-            take = functools.partial(lambda ref, i: ref[i : i + 1], these["a"])
-            source = squeeze(level, [take], (None,))[0]
-
-    for way in AROUND:
+        own, total = sums(level, pad)
+        these["a"][...] = jnp.where(red_cells, these["diag"][...] * (total - own), 0.0)
+        take = functools.partial(lambda ref, i: ref[i : i + 1], these["a"])
+        source = squeeze(level, [take], (None,))[0]
+    wide_level(source)
+
+    for way in WIDE:
         chosen = [key for key in keys if key[2] == way]
 
         @pl.when(inside(*way))
@@ -420,12 +507,16 @@
         copy.wait()
 
 
-def store(fine, middle, coarse, fine_out, middle_out, coarse_out, sem):
-    pairs = ((fine, fine_out), (middle, middle_out), (coarse, coarse_out))
-    copies = [pltpu.make_async_copy(src, dst, sem.at[n]) for n, (src, dst) in enumerate(pairs)]
-    for copy in copies:
+def store(*refs):
+    given, outs, held, sem = refs[:3], refs[3:6], refs[6:9], refs[9]
+    loads = [pltpu.make_async_copy(given[n], held[n], sem.at[n]) for n in range(3)]
+    stores = [pltpu.make_async_copy(held[n], outs[n], sem.at[3 + n]) for n in range(3)]
+    for copy in loads:
         copy.start()
-    for copy in copies:
+    for load, copy in zip(loads, stores):
+        load.wait()
+        copy.start()
+    for copy in stores:
         copy.wait()
 
 
@@ -448,6 +539,7 @@
     for nx, ny, nz in dims_of[:2]:
         scratch += [pltpu.VMEM((4 * nx // 2, 8, nz), jnp.float32)]
     scratch += [pltpu.SemaphoreType.DMA((len(keys),))] * 2
+    scratch += [pltpu.VMEM((8, 8, dims_of[-1][2]), jnp.float32)] * 12
     iterates = pl.pallas_call(
         functools.partial(kernel, dims_of, keys),
         out_shape=[jax.ShapeDtypeStruct(dims, jnp.float32) for dims in dims_of],
@@ -464,7 +556,8 @@
         out_shape=[jax.ShapeDtypeStruct(dims, jnp.float32) for dims in dims_of],
         in_specs=[pl.BlockSpec(memory_space=pltpu.HBM)] * 3,
         out_specs=[pl.BlockSpec(memory_space=pltpu.HBM)] * 3,
-        scratch_shapes=[pltpu.SemaphoreType.DMA((3,))],
+        scratch_shapes=[pltpu.VMEM(dims, jnp.float32) for dims in dims_of]
+        + [pltpu.SemaphoreType.DMA((6,))],
         compiler_params=pltpu.CompilerParams(vmem_limit_bytes=VMEM_LIMIT),
         name="store",
     )(*iterates)

time: 36.7 us -> 30.2 us (0.82)
  Pallas kernels: 35.9 us -> 29.4 us
    pallas_call x1, Pallas kernels: 5.66 us -> 1.62 us  [shards(): pl.pallas_call(store, out_shape=[jax.ShapeDtypeStruct(dims, jnp.float32)...]
    pallas_call x1, Pallas kernels: 30.3 us -> 27.8 us  [shards(): pl.pallas_call(functools.partial(kernel, dims_of, keys), out_shape=[jax.S...]
where the time goes in v3:
time: 30.2 us; the launch traced here: 30 us
  Pallas kernels  29.4 us (97%)
  between operations  0.64 us (2%)
    pallas_call x1, Pallas kernels, shards(): pl.pallas_call(functools.partial(kernel, dims_of, keys), out_shape=[jax.S...  27.8 us
    pallas_call x1, Pallas kernels, shards(): pl.pallas_call(store, out_shape=[jax.ShapeDtypeStruct(dims, jnp.float32)...  1.62 us

profile of v3, /device:TPU:0, one launch (start us, length us, event | category | flops | bytes accessed | tf_op | source)
XLA Modules:
  0.0 30.0 jit_solution(3694222555258427532)
XLA Ops:
  0.6 27.8 %vcycle.1 = (f32[8,8,512]{2,1,0:T(8,128)}, f32[4,4,256]{2,1,0:T(4,128)}, f32[2,2,128]{2,1,0:T(2,128)}) custom-call(f32[8,8,512]{2,1,0:T(8,128)} %refs_0_.1, f32[8,8,512]{2,1,0:T(8,128)} %refs_1_.1, bf16[8,8,512]{2,1,0:T(8,128)(2,1)} %refs_2_.1, bf16[8,8,512]{2,1,0:T(8,128)(2,1)} %refs_3_.1, bf16[8,8,512]{2,1,0:T(8,128)(2,1)} %refs_4_.1, ...), custom_call_target="tpu_custom_call" | custom-call | tf_op jit(solution)/shard_map/vcycle/pallas_call | solution.py:543
  28.4 1.6 %store.1 = (f32[8,8,512]{2,1,0:T(8,128)}, f32[4,4,256]{2,1,0:T(4,128)}, f32[2,2,128]{2,1,0:T(2,128)}) custom-call(f32[8,8,512]{2,1,0:T(8,128)} %get-tuple-element.6.refs_0_, f32[4,4,256]{2,1,0:T(4,128)} %get-tuple-element.7.refs_1_, f32[2,2,128]{2,1,0:T(2,128)} %get-tuple-element.8.refs_2_), custom_call_target="tpu_custom_call" | custom-call | tf_op jit(solution)/shard_map/store/pallas_call | solution.py:554

commit v4 on v2

--- a/solution.py
+++ b/solution.py
@@ -14,6 +14,25 @@
 FACES = ((1, 0), (-1, 0), (0, 1), (0, -1))
 CORNERS = ((1, 1), (1, -1), (-1, 1), (-1, -1))
 AROUND = FACES + CORNERS
+FAR = ((2, 0), (-2, 0), (0, 2), (0, -2))
+WIDE = AROUND + FAR
+WIDE_NAMES = ("a", "bx", "by", "bz", "g", "over", "xu", "xl", "yu", "yl", "zu", "zl")
+REACH = {1: 4, 2: 3}
+ROWS = {1: 16, 2: 8}
+WAYS = {1: AROUND, 2: WIDE}
+
+
+def box(kind, level, way, dims):
+    nx, ny, _ = dims
+    if level == 2:
+        return slice(0, nx), slice(0, ny)
+    if kind == "source":
+        xs = {0: (0, nx), 1: (1 if way[1] else 0, nx), -1: (0, 3 if way[1] else nx)}[way[0]]
+        return slice(*xs), slice(0, ny)
+    corner = way[0] != 0 and way[1] != 0
+    least = {0: 0, 1: 1 if corner else 0, -1: 0}
+    most = {0: 4, 1: 4, -1: 2 if way == (-1, -1) else 3}
+    return slice(least[way[0]], most[way[0]]), slice(least[way[1]], most[way[1]])
 
 
 def layer_shape(dims, way):
@@ -29,16 +48,20 @@
     found = {}
     for way in FACES:
         found[("first", 0, way)] = layer_shape(dims_of[0], way)
-    for level, dims in enumerate(dims_of):
-        for way in ((1, 0), (0, 1)):
-            found[("lower", level, way)] = layer_shape(dims, way)
-        for way in FACES:
-            found[("toward", level, way)] = layer_shape(dims, way)
-            found[("ends", level, way)] = edge_shape(dims, way)
-        for half in range(2):
-            ways = FACES if (level == LEVELS - 1 and half == 1) else AROUND
-            for way in ways:
-                found[("half%d" % half, level, way)] = layer_shape(dims, way)
+    for level in REACH:
+        nx, ny, nz = dims_of[level]
+        for way in WAYS[level]:
+            found[("raw", level, way)] = (nx, ny, 4, nz)
+            found[("source", level, way)] = (nx, ny, nz)
+    dims = dims_of[0]
+    for way in ((1, 0), (0, 1)):
+        found[("lower", 0, way)] = layer_shape(dims, way)
+    for way in FACES:
+        found[("toward", 0, way)] = layer_shape(dims, way)
+        found[("ends", 0, way)] = edge_shape(dims, way)
+    for half in range(2):
+        for way in AROUND:
+            found[("half%d" % half, 0, way)] = layer_shape(dims, way)
     return found
 
 
@@ -79,12 +102,14 @@
     in_buf = dict(zip(keys, refs[n_keys : 2 * n_keys]))
     refs = refs[2 * n_keys :]
     names = ("open", "shut", "g", "diag", "xu", "xl", "yu", "yl", "zu", "zl", "a", "bx", "by", "bz")
-    per = []
-    for level in range(LEVELS):
-        per.append(dict(zip(names, refs[: len(names)])))
-        refs = refs[len(names) :]
+    per = [dict(zip(names, refs[:14]))]
+    refs = refs[14:]
+    for level in REACH:
+        per.append(dict(zip(names[-4:], refs[:4])))
+        refs = refs[4:]
     pair_t, cols_t = refs[0:2], refs[2:4]
     send_sem, recv_sem = refs[4], refs[5]
+    wides = {1: dict(zip(WIDE_NAMES, refs[6:18])), 2: dict(zip(WIDE_NAMES, refs[18:30]))}
 
     gx, gy = lax.axis_index("gx"), lax.axis_index("gy")
     n_x, n_y = lax.axis_size("gx"), lax.axis_size("gy")
@@ -101,9 +126,13 @@
     def copy_of(key):
         way = key[2]
         index = keys.index(key)
+        src, dst = out_buf[key], in_buf[key]
+        if key[0] in ("raw", "source"):
+            xs, ys = box(*key, dims_of[key[1]])
+            src, dst = out_buf[key[:2] + WIDE[:1]].at[xs, ys], dst.at[xs, ys]
         return pltpu.make_async_remote_copy(
-            src_ref=out_buf[key],
-            dst_ref=in_buf[key],
+            src_ref=src,
+            dst_ref=dst,
             send_sem=send_sem.at[index],
             recv_sem=recv_sem.at[index],
             device_id={"gx": gx + way[0], "gy": gy + way[1]},
@@ -111,7 +140,7 @@
         )
 
     def send(group):
-        for way in AROUND:
+        for way in WIDE:
             chosen = [key for key in group if key[2] == way]
             if chosen:
 
@@ -121,7 +150,7 @@
                         copy_of(key).start()
 
     def receive(group):
-        for way in AROUND:
+        for way in WIDE:
             chosen = [key for key in group if key[2] == way]
             if chosen:
 
@@ -137,7 +166,7 @@
     loads = [pltpu.make_async_copy(args[n], held[n], load_sem.at[n]) for n in range(6)]
 
     barrier = pltpu.get_barrier_semaphore()
-    for way in AROUND:
+    for way in WIDE:
 
         @pl.when(inside(*way))
         def _():
@@ -171,7 +200,7 @@
     put_lower(0)
 
     for way in AROUND:
-        chosen = [key for key in keys if key[2] == way]
+        chosen = [key for key in keys if key[2] == way and key[0] not in ("raw", "source")]
 
         @pl.when(jnp.logical_not(inside(-way[0], -way[1])))
         def _():
@@ -180,7 +209,9 @@
 
     beside_x = (gx > 0).astype(jnp.int32) + (gx + 1 < n_x).astype(jnp.int32)
     beside_y = (gy > 0).astype(jnp.int32) + (gy + 1 < n_y).astype(jnp.int32)
-    pl.semaphore_wait(barrier, beside_x + beside_y + beside_x * beside_y)
+    far_x = (gx > 1).astype(jnp.int32) + (gx + 2 < n_x).astype(jnp.int32)
+    far_y = (gy > 1).astype(jnp.int32) + (gy + 2 < n_y).astype(jnp.int32)
+    pl.semaphore_wait(barrier, beside_x + beside_y + beside_x * beside_y + far_x + far_y)
 
     send(group_of("first", 0) + group_of("lower", 0))
     loads[2].wait()
@@ -240,11 +271,6 @@
         ]
         for name, v in zip(names, squeeze(level, sources, (None, 0, 1, 2))):
             per[level + 1][name][...] = v
-
-    for level in range(1, LEVELS):
-        coarse_coefs(level - 1)
-        put_lower(level)
-        send(group_of("lower", level))
 
     def make_coefs(level):
         these = per[level]
@@ -366,66 +392,205 @@
             theirs = in_buf[(kind, level, back(way))][...]
             pad[px, py, :] = pad[px, py, :] + out_buf[("toward", level, way)][...] * theirs
 
-    for level in range(LEVELS):
-        these = per[level]
-        nx, ny, nz = dims_of[level]
-        these["shut"][...] = jnp.zeros(these["shut"].shape, jnp.float32)
-
-    source = None
-    for level in range(LEVELS):
-        these = per[level]
-        dims = dims_of[level]
-        nx, ny, nz = dims
-        pad = these["open"]
-        red_cells = jnp.logical_not(parity_at(dims))
-        if level == 0:
-            receive(group_of("lower", 0))
-            these["g"][...] = f_in[...] * make_coefs(0)
-            receive(group_of("first", 0))
-            pad[1 : 1 + nx, ROW : ROW + ny, :] = u_in[...]
-            for way in FACES:
-                hx, hy = halo_place(dims, way)
-                pad[hx, hy, :] = in_buf[("first", 0, (-way[0], -way[1]))][...]
-            own, total = sums(0, pad)
-            half_sweep(0, 0, jnp.where(red_cells, total, own))
-            put_toward(0)
-            for other in range(1, LEVELS):
-                receive(group_of("lower", other))
-                per[other]["g"][...] = make_coefs(other)
-                put_toward(other)
+    def put_raw(level):
+        buffer = out_buf[("raw", level, WIDE[0])]
+        for c, name in enumerate(WIDE_NAMES[:4]):
+            for y in range(dims_of[level][1]):
+                buffer[:, y, c : c + 1, :] = per[level][name][:, y : y + 1, :]
+
+    def spread(kind, level, ways, targets):
+        nx, ny, _ = dims_of[level]
+        reach = REACH[level]
+        for way in ways:
+            key = (kind, level, way)
+            at_x, at_y = -nx * way[0], -ny * way[1]
+            xs, ys = box(*key, dims_of[level])
+            x_from, x_to = max(xs.start, -reach - at_x), min(xs.stop, nx + reach - at_x)
+            y_from = max(ys.start, -reach - at_y)
+            y_to = min(ys.stop, ny + reach - at_y)
+            to = (at_y + y_from) % ROWS[level]
+            planes = slice(at_x + x_from + reach, at_x + x_to + reach)
+
+            @pl.when(inside(-way[0], -way[1]))
+            def _():
+                copy_of(key).wait_recv()
+                if len(targets) == 1:
+                    targets[0][planes, to : to + y_to - y_from, :] = in_buf[key][
+                        x_from:x_to, y_from:y_to, :
+                    ]
+                else:
+                    for c, target in enumerate(targets):
+                        for y in range(y_from, y_to):
+                            row = to + y - y_from
+                            target[planes, row : row + 1, :] = in_buf[key][
+                                x_from:x_to, y, c : c + 1, :
+                            ]
+
+    def lower_x(v):
+        return jnp.concatenate([jnp.zeros_like(v[:1]), v[:-1]], axis=0)
+
+    def wide_start(level):
+        nx, ny, _ = dims_of[level]
+        wide, reach = wides[level], REACH[level]
+        for name in WIDE_NAMES[:5]:
+            wide[name][...] = jnp.zeros(wide[name].shape, jnp.float32)
+        for name in WIDE_NAMES[:4]:
+            wide[name][reach : reach + nx, 0:ny, :] = per[level][name][...]
+
+    def wide_diag(level, xs):
+        wide = wides[level]
+        scale = 0.25**level
+        a, bx, by, bz = (wide[name][xs] for name in WIDE_NAMES[:4])
+        place = lax.broadcasted_iota(jnp.int32, a.shape, 2)
+        if xs.start > 0:
+            bxl = wide["bx"][xs.start - 1 : xs.stop - 1]
         else:
-            these["g"][...] = source * these["g"][...]
-            half_sweep(level, 0, jnp.where(red_cells, these["g"][...], 0.0))
-        finish_half(level, 0, False)
-        own, total = sums(level, pad)
-        half_sweep(level, 1, jnp.where(red_cells, total, own))
-        finish_half(level, 1, level == LEVELS - 1)
-        kept[level][...] = pad[1 : 1 + nx, ROW : ROW + ny, :]
-        stores[level].start()
-        if level + 1 < LEVELS:
-            own, total = sums(level, pad)
-            these["a"][...] = jnp.where(red_cells, these["diag"][...] * (total - own), 0.0)
-            take = functools.partial(lambda ref, i: ref[i : i + 1], these["a"])
-            source = squeeze(level, [take], (None,))[0]
-
-    for way in AROUND:
-        chosen = [key for key in keys if key[2] == way]
-
-        @pl.when(inside(*way))
-        def _():
-            for key in chosen:
-                copy_of(key).wait_send()
+            bxl = lower_x(bx)
+        byl = pltpu.roll(by, 1, 1)
+        bzl = jnp.where(place == 0, 0.0, pltpu.roll(bz, 1, 2))
+        diag = a + scale * ((bx + bxl) + (by + byl) + (bz + bzl))
+        over = jnp.where(a > 0.0, 1.0 / jnp.where(a > 0.0, diag, 1.0), 0.0)
+        return diag, over, (bx, bxl, by, byl, bz, bzl)
+
+    def wide_coefs(level):
+        wide = wides[level]
+        nz = dims_of[level][2]
+        planes = wide["a"].shape[0]
+        _, over, faces = wide_diag(level, slice(0, planes))
+        over = over * 0.25**level
+        bx, bxl, by, byl, bz, bzl = faces
+        place = lax.broadcasted_iota(jnp.int32, bz.shape, 2)
+        wide["xu"][...], wide["xl"][...] = bx * over, bxl * over
+        wide["yu"][...], wide["yl"][...] = by * over, byl * over
+        wide["zu"][...] = jnp.where(place == nz - 1, 0.0, bz * over)
+        wide["zl"][...] = bzl * over
+
+    def wide_sums(level, u, xs):
+        wide = wides[level]
+        nz, rows = dims_of[level][2], ROWS[level]
+        own = u[1:-1]
+        total = wide["g"][xs] + wide["xu"][xs] * u[2:] + wide["xl"][xs] * u[:-2]
+        total = total + wide["yu"][xs] * pltpu.roll(own, rows - 1, 1)
+        total = total + wide["yl"][xs] * pltpu.roll(own, 1, 1)
+        total = total + wide["zu"][xs] * pltpu.roll(own, nz - 1, 2)
+        total = total + wide["zl"][xs] * pltpu.roll(own, 1, 2)
+        return own, total
+
+    def wide_send(level, source):
+        nx, ny, _ = dims_of[level]
+        wide, reach = wides[level], REACH[level]
+        own = source * wide["over"][reach : reach + nx, 0:ny, :]
+        out_buf[("source", level, WIDE[0])][...] = own
+        send(group_of("source", level))
+        wide["g"][reach : reach + nx, 0:ny, :] = own
+
+    def wide_smooth(level):
+        nx, ny, _ = dims_of[level]
+        reach = REACH[level]
+        spread("source", level, WAYS[level], [wides[level]["g"]])
+        g = wides[level]["g"][...]
+        u = jnp.where(parity_at(g.shape, reach), 0.0, g)
+        first = reach - 3
+        if first == 0:
+            edge = jnp.zeros_like(u[:1])
+            u = jnp.concatenate([edge, u, edge], axis=0)
+        for step in range(3):
+            xs = slice(first, nx + 2 * reach - first)
+            own, total = wide_sums(level, u, xs)
+            black = parity_at(total.shape, reach + first)
+            u = jnp.where(black, own, total) if step == 1 else jnp.where(black, total, own)
+            first += 1
+        return u
+
+    dims = dims_of[0]
+    nx, ny, nz = dims
+    these = per[0]
+    pad = these["open"]
+    these["shut"][...] = jnp.zeros(these["shut"].shape, jnp.float32)
+    red_cells = jnp.logical_not(parity_at(dims))
+    receive(group_of("lower", 0))
+    these["g"][...] = f_in[...] * make_coefs(0)
+    receive(group_of("first", 0))
+    pad[1 : 1 + nx, ROW : ROW + ny, :] = u_in[...]
+    for way in FACES:
+        hx, hy = halo_place(dims, way)
+        pad[hx, hy, :] = in_buf[("first", 0, (-way[0], -way[1]))][...]
+    own, total = sums(0, pad)
+    half_sweep(0, 0, jnp.where(red_cells, total, own))
+    put_toward(0)
+    coarse_coefs(0)
+    put_raw(1)
+    send([key for key in group_of("raw", 1) if key[2] in FACES])
+    coarse_coefs(1)
+    put_raw(2)
+    send(group_of("raw", 2))
+    wide_start(1)
+    finish_half(0, 0, False)
+    own, total = sums(0, pad)
+    half_sweep(0, 1, jnp.where(red_cells, total, own))
+    send([key for key in group_of("raw", 1) if key[2] in CORNERS])
+    spread("raw", 1, FACES, [wides[1][name] for name in WIDE_NAMES[:4]])
+    middle = slice(REACH[1], REACH[1] + dims_of[1][0])
+    diag, over, _ = wide_diag(1, middle)
+    middle_diag = per[1]["bx"]
+    middle_diag[...] = diag[:, 0 : dims_of[1][1], :]
+    wides[1]["over"][middle] = over
+    finish_half(0, 1, False)
+    kept[0][...] = pad[1 : 1 + nx, ROW : ROW + ny, :]
+    stores[0].start()
+    own, total = sums(0, pad)
+    these["a"][...] = jnp.where(red_cells, these["diag"][...] * (total - own), 0.0)
+    take = functools.partial(lambda ref, i: ref[i : i + 1], these["a"])
+    wide_send(1, squeeze(0, [take], (None,))[0])
+
+    spread("raw", 1, CORNERS, [wides[1][name] for name in WIDE_NAMES[:4]])
+    wide_coefs(1)
+    wide_start(2)
+    spread("raw", 2, WAYS[2], [wides[2][name] for name in WIDE_NAMES[:4]])
+    _, over, _ = wide_diag(2, slice(0, wides[2]["a"].shape[0]))
+    wides[2]["over"][...] = over
+    wide_coefs(2)
+    u = wide_smooth(1)
+    ny = dims_of[1][1]
+    kept[1][...] = u[1:-1, 0:ny, :]
+    stores[1].start()
+    own, total = wide_sums(1, u, middle)
+    red_cells = jnp.logical_not(parity_at(dims_of[1]))
+    per[1]["a"][...] = jnp.where(
+        red_cells, middle_diag[...] * (total[:, 0:ny, :] - own[:, 0:ny, :]), 0.0
+    )
+    take = functools.partial(lambda ref, i: ref[i : i + 1], per[1]["a"])
+    wide_send(2, squeeze(1, [take], (None,))[0])
+
+    def sent(chosen_of):
+        for way in WIDE:
+            chosen = [key for key in keys if key[2] == way and chosen_of(key)]
+
+            @pl.when(inside(*way))
+            def _():
+                for key in chosen:
+                    copy_of(key).wait_send()
+
+    sent(lambda key: key[:2] != ("source", 2))
+    u = wide_smooth(2)
+    kept[2][...] = u[1:-1, 0 : dims_of[2][1], :]
+    stores[2].start()
+    sent(lambda key: key[:2] == ("source", 2))
 
     for copy in stores:
         copy.wait()
 
 
-def store(fine, middle, coarse, fine_out, middle_out, coarse_out, sem):
-    pairs = ((fine, fine_out), (middle, middle_out), (coarse, coarse_out))
-    copies = [pltpu.make_async_copy(src, dst, sem.at[n]) for n, (src, dst) in enumerate(pairs)]
-    for copy in copies:
+def store(*refs):
+    given, outs, held, sem = refs[:3], refs[3:6], refs[6:9], refs[9]
+    loads = [pltpu.make_async_copy(given[n], held[n], sem.at[n]) for n in range(3)]
+    stores = [pltpu.make_async_copy(held[n], outs[n], sem.at[3 + n]) for n in range(3)]
+    for copy in loads:
         copy.start()
-    for copy in copies:
+    for load, copy in zip(loads, stores):
+        load.wait()
+        copy.start()
+    for copy in stores:
         copy.wait()
 
 
@@ -439,15 +604,19 @@
     scratch += [pltpu.SemaphoreType.DMA((6,)), pltpu.SemaphoreType.DMA((LEVELS,))]
     scratch += [pltpu.VMEM(dims, jnp.float32) for dims in dims_of]
     scratch += buffers + buffers
-    for nx, ny, nz in dims_of:
-        rows = 24 if ny + 1 > 8 else 16
-        scratch += [pltpu.VMEM((nx + 2, rows, nz), jnp.float32)] * 2
-        scratch += [pltpu.VMEM((nx, ny, nz), jnp.float32)] * 12
+    nx, ny, nz = fine
+    scratch += [pltpu.VMEM((nx + 2, 24, nz), jnp.float32)] * 2
+    scratch += [pltpu.VMEM(fine, jnp.float32)] * 12
+    for level in REACH:
+        scratch += [pltpu.VMEM(dims_of[level], jnp.float32)] * 4
     for nx, ny, nz in dims_of[:2]:
         scratch += [pltpu.VMEM((4 * nx // 2, ny, nz), jnp.float32)]
     for nx, ny, nz in dims_of[:2]:
         scratch += [pltpu.VMEM((4 * nx // 2, 8, nz), jnp.float32)]
     scratch += [pltpu.SemaphoreType.DMA((len(keys),))] * 2
+    for level, reach in REACH.items():
+        nx, _, nz = dims_of[level]
+        scratch += [pltpu.VMEM((nx + 2 * reach, ROWS[level], nz), jnp.float32)] * 12
     iterates = pl.pallas_call(
         functools.partial(kernel, dims_of, keys),
         out_shape=[jax.ShapeDtypeStruct(dims, jnp.float32) for dims in dims_of],
@@ -464,7 +633,8 @@
         out_shape=[jax.ShapeDtypeStruct(dims, jnp.float32) for dims in dims_of],
         in_specs=[pl.BlockSpec(memory_space=pltpu.HBM)] * 3,
         out_specs=[pl.BlockSpec(memory_space=pltpu.HBM)] * 3,
-        scratch_shapes=[pltpu.SemaphoreType.DMA((3,))],
+        scratch_shapes=[pltpu.VMEM(dims, jnp.float32) for dims in dims_of]
+        + [pltpu.SemaphoreType.DMA((6,))],
         compiler_params=pltpu.CompilerParams(vmem_limit_bytes=VMEM_LIMIT),
         name="store",
     )(*iterates)

time: 36.7 us -> 28.9 us (0.79)
  Pallas kernels: 35.9 us -> 28.1 us
    pallas_call x1, Pallas kernels: 5.66 us -> 1.62 us  [shards(): pl.pallas_call(store, out_shape=[jax.ShapeDtypeStruct(dims, jnp.float32)...]
    pallas_call x1, Pallas kernels: 30.3 us -> 26.5 us  [shards(): pl.pallas_call(functools.partial(kernel, dims_of, keys), out_shape=[jax.S...]
where the time goes in v4:
time: 28.9 us; the launch traced here: 28.7 us
  Pallas kernels  28.1 us (97%)
  between operations  0.64 us (2%)
    pallas_call x1, Pallas kernels, shards(): pl.pallas_call(functools.partial(kernel, dims_of, keys), out_shape=[jax.S...  26.5 us
    pallas_call x1, Pallas kernels, shards(): pl.pallas_call(store, out_shape=[jax.ShapeDtypeStruct(dims, jnp.float32)...  1.62 us

profile of v4, /device:TPU:0, one launch (start us, length us, event | category | flops | bytes accessed | tf_op | source)
XLA Modules:
  0.0 28.7 jit_solution(8400160819785486453)
XLA Ops:
  0.6 26.5 %vcycle.1 = (f32[8,8,512]{2,1,0:T(8,128)}, f32[4,4,256]{2,1,0:T(4,128)}, f32[2,2,128]{2,1,0:T(2,128)}) custom-call(f32[8,8,512]{2,1,0:T(8,128)} %refs_0_.1, f32[8,8,512]{2,1,0:T(8,128)} %refs_1_.1, bf16[8,8,512]{2,1,0:T(8,128)(2,1)} %refs_2_.1, bf16[8,8,512]{2,1,0:T(8,128)(2,1)} %refs_3_.1, bf16[8,8,512]{2,1,0:T(8,128)(2,1)} %refs_4_.1, ...), custom_call_target="tpu_custom_call" | custom-call | tf_op jit(solution)/shard_map/vcycle/pallas_call | solution.py:620
  27.1 1.6 %store.1 = (f32[8,8,512]{2,1,0:T(8,128)}, f32[4,4,256]{2,1,0:T(4,128)}, f32[2,2,128]{2,1,0:T(2,128)}) custom-call(f32[8,8,512]{2,1,0:T(8,128)} %get-tuple-element.6.refs_0_, f32[4,4,256]{2,1,0:T(4,128)} %get-tuple-element.7.refs_1_, f32[2,2,128]{2,1,0:T(2,128)} %get-tuple-element.8.refs_2_), custom_call_target="tpu_custom_call" | custom-call | tf_op jit(solution)/shard_map/store/pallas_call | solution.py:631

commit v5 on v4

--- a/solution.py
+++ b/solution.py
@@ -11,7 +11,7 @@
 VMEM_LIMIT = (64 * 1024 - 160) * 1024
 ROW = 8
 
-FACES = ((1, 0), (-1, 0), (0, 1), (0, -1))
+FACES = ((0, 1), (0, -1), (1, 0), (-1, 0))
 CORNERS = ((1, 1), (1, -1), (-1, 1), (-1, -1))
 AROUND = FACES + CORNERS
 FAR = ((2, 0), (-2, 0), (0, 2), (0, -2))
@@ -110,6 +110,7 @@
     pair_t, cols_t = refs[0:2], refs[2:4]
     send_sem, recv_sem = refs[4], refs[5]
     wides = {1: dict(zip(WIDE_NAMES, refs[6:18])), 2: dict(zip(WIDE_NAMES, refs[18:30]))}
+    pairs = refs[30]
 
     gx, gy = lax.axis_index("gx"), lax.axis_index("gy")
     n_x, n_y = lax.axis_size("gx"), lax.axis_size("gy")
@@ -185,6 +186,15 @@
             xs, ys = at_side(dims_of[level], way)
             out_buf[(kind, level, way)][...] = source[xs, ys, :]
 
+    size = pairs.shape[0]
+    row = lax.broadcasted_iota(jnp.int32, (size, size // 2), 0)
+    column = lax.broadcasted_iota(jnp.int32, (size, size // 2), 1)
+    pairs[...] = jnp.where((row >> 1) == column, 1.0, 0.0).astype(jnp.bfloat16)
+    for level in REACH:
+        for name in WIDE_NAMES[:5]:
+            wides[level][name][...] = jnp.zeros(wides[level][name].shape, jnp.float32)
+    per[0]["shut"][...] = jnp.zeros(per[0]["shut"].shape, jnp.float32)
+
     loads[0].wait()
     put_faces("first", 0, u_in, FACES)
 
@@ -220,11 +230,6 @@
     per[0]["bz"][...] = bz_in[...].astype(jnp.float32)
     loads[1].wait()
 
-    def pair_matrix(size):
-        fine = lax.broadcasted_iota(jnp.int32, (size, size // 2), 0)
-        coarse = lax.broadcasted_iota(jnp.int32, (size, size // 2), 1)
-        return jnp.where((fine >> 1) == coarse, 1.0, 0.0).astype(jnp.bfloat16)
-
     def three(v):
         high = v.astype(jnp.bfloat16)
         rest = v - high.astype(jnp.float32)
@@ -235,7 +240,7 @@
     def sum_pairs_z(v):
         rows, size = v.shape
         parts = jnp.concatenate(three(v), axis=0)
-        got = jnp.dot(parts, pair_matrix(size), preferred_element_type=jnp.float32)
+        got = jnp.dot(parts, pairs[0:size, 0 : size // 2], preferred_element_type=jnp.float32)
         return got[:rows] + got[rows : 2 * rows] + got[2 * rows :]
 
     def squeeze(level, sources, ways):
@@ -432,8 +437,6 @@
     def wide_start(level):
         nx, ny, _ = dims_of[level]
         wide, reach = wides[level], REACH[level]
-        for name in WIDE_NAMES[:5]:
-            wide[name][...] = jnp.zeros(wide[name].shape, jnp.float32)
         for name in WIDE_NAMES[:4]:
             wide[name][reach : reach + nx, 0:ny, :] = per[level][name][...]
 
@@ -506,8 +509,10 @@
     nx, ny, nz = dims
     these = per[0]
     pad = these["open"]
-    these["shut"][...] = jnp.zeros(these["shut"].shape, jnp.float32)
     red_cells = jnp.logical_not(parity_at(dims))
+    coarse_coefs(0)
+    put_raw(1)
+    wide_start(1)
     receive(group_of("lower", 0))
     these["g"][...] = f_in[...] * make_coefs(0)
     receive(group_of("first", 0))
@@ -518,13 +523,11 @@
     own, total = sums(0, pad)
     half_sweep(0, 0, jnp.where(red_cells, total, own))
     put_toward(0)
-    coarse_coefs(0)
-    put_raw(1)
     send([key for key in group_of("raw", 1) if key[2] in FACES])
     coarse_coefs(1)
     put_raw(2)
     send(group_of("raw", 2))
-    wide_start(1)
+    wide_start(2)
     finish_half(0, 0, False)
     own, total = sums(0, pad)
     half_sweep(0, 1, jnp.where(red_cells, total, own))
@@ -535,6 +538,10 @@
     middle_diag = per[1]["bx"]
     middle_diag[...] = diag[:, 0 : dims_of[1][1], :]
     wides[1]["over"][middle] = over
+    spread("raw", 2, WAYS[2], [wides[2][name] for name in WIDE_NAMES[:4]])
+    _, over, _ = wide_diag(2, slice(0, wides[2]["a"].shape[0]))
+    wides[2]["over"][...] = over
+    wide_coefs(2)
     finish_half(0, 1, False)
     kept[0][...] = pad[1 : 1 + nx, ROW : ROW + ny, :]
     stores[0].start()
@@ -545,11 +552,6 @@
 
     spread("raw", 1, CORNERS, [wides[1][name] for name in WIDE_NAMES[:4]])
     wide_coefs(1)
-    wide_start(2)
-    spread("raw", 2, WAYS[2], [wides[2][name] for name in WIDE_NAMES[:4]])
-    _, over, _ = wide_diag(2, slice(0, wides[2]["a"].shape[0]))
-    wides[2]["over"][...] = over
-    wide_coefs(2)
     u = wide_smooth(1)
     ny = dims_of[1][1]
     kept[1][...] = u[1:-1, 0:ny, :]
@@ -617,6 +619,7 @@
     for level, reach in REACH.items():
         nx, _, nz = dims_of[level]
         scratch += [pltpu.VMEM((nx + 2 * reach, ROWS[level], nz), jnp.float32)] * 12
+    scratch += [pltpu.VMEM((fine[2], fine[2] // 2), jnp.bfloat16)]
     iterates = pl.pallas_call(
         functools.partial(kernel, dims_of, keys),
         out_shape=[jax.ShapeDtypeStruct(dims, jnp.float32) for dims in dims_of],

time: 28.9 us -> 28.8 us (level)
  no operation moved by 1% of the time
where the time goes in v5:
time: 28.8 us; the launch traced here: 28.7 us
  Pallas kernels  28 us (97%)
  between operations  0.64 us (2%)
    pallas_call x1, Pallas kernels, shards(): pl.pallas_call(functools.partial(kernel, dims_of, keys), out_shape=[jax.S...  26.4 us
    pallas_call x1, Pallas kernels, shards(): pl.pallas_call(store, out_shape=[jax.ShapeDtypeStruct(dims, jnp.float32)...  1.62 us

profile of v5, /device:TPU:0, one launch (start us, length us, event | category | flops | bytes accessed | tf_op | source)
XLA Modules:
  0.0 28.7 jit_solution(10922520718637173218)
XLA Ops:
  0.6 26.4 %vcycle.1 = (f32[8,8,512]{2,1,0:T(8,128)}, f32[4,4,256]{2,1,0:T(4,128)}, f32[2,2,128]{2,1,0:T(2,128)}) custom-call(f32[8,8,512]{2,1,0:T(8,128)} %refs_0_.1, f32[8,8,512]{2,1,0:T(8,128)} %refs_1_.1, bf16[8,8,512]{2,1,0:T(8,128)(2,1)} %refs_2_.1, bf16[8,8,512]{2,1,0:T(8,128)(2,1)} %refs_3_.1, bf16[8,8,512]{2,1,0:T(8,128)(2,1)} %refs_4_.1, ...), custom_call_target="tpu_custom_call" | custom-call | tf_op jit(solution)/shard_map/vcycle/pallas_call | solution.py:623
  27.1 1.6 %store.1 = (f32[8,8,512]{2,1,0:T(8,128)}, f32[4,4,256]{2,1,0:T(4,128)}, f32[2,2,128]{2,1,0:T(2,128)}) custom-call(f32[8,8,512]{2,1,0:T(8,128)} %get-tuple-element.6.refs_0_, f32[4,4,256]{2,1,0:T(4,128)} %get-tuple-element.7.refs_1_, f32[2,2,128]{2,1,0:T(2,128)} %get-tuple-element.8.refs_2_), custom_call_target="tpu_custom_call" | custom-call | tf_op jit(solution)/shard_map/store/pallas_call | solution.py:634

commit v6 on v5

--- a/solution.py
+++ b/solution.py
@@ -223,7 +223,8 @@
     far_y = (gy > 1).astype(jnp.int32) + (gy + 2 < n_y).astype(jnp.int32)
     pl.semaphore_wait(barrier, beside_x + beside_y + beside_x * beside_y + far_x + far_y)
 
-    send(group_of("first", 0) + group_of("lower", 0))
+    send(group_of("lower", 0))
+    send(group_of("first", 0))
     loads[2].wait()
     per[0]["a"][...] = a_in[...].astype(jnp.float32)
     loads[5].wait()
@@ -512,9 +513,11 @@
     red_cells = jnp.logical_not(parity_at(dims))
     coarse_coefs(0)
     put_raw(1)
+    send([key for key in group_of("raw", 1) if key[2] in FACES])
     wide_start(1)
     receive(group_of("lower", 0))
     these["g"][...] = f_in[...] * make_coefs(0)
+    put_toward(0)
     receive(group_of("first", 0))
     pad[1 : 1 + nx, ROW : ROW + ny, :] = u_in[...]
     for way in FACES:
@@ -522,26 +525,20 @@
         pad[hx, hy, :] = in_buf[("first", 0, (-way[0], -way[1]))][...]
     own, total = sums(0, pad)
     half_sweep(0, 0, jnp.where(red_cells, total, own))
-    put_toward(0)
-    send([key for key in group_of("raw", 1) if key[2] in FACES])
+    send([key for key in group_of("raw", 1) if key[2] in CORNERS])
     coarse_coefs(1)
     put_raw(2)
-    send(group_of("raw", 2))
     wide_start(2)
     finish_half(0, 0, False)
     own, total = sums(0, pad)
     half_sweep(0, 1, jnp.where(red_cells, total, own))
-    send([key for key in group_of("raw", 1) if key[2] in CORNERS])
+    send(group_of("raw", 2))
     spread("raw", 1, FACES, [wides[1][name] for name in WIDE_NAMES[:4]])
     middle = slice(REACH[1], REACH[1] + dims_of[1][0])
     diag, over, _ = wide_diag(1, middle)
     middle_diag = per[1]["bx"]
     middle_diag[...] = diag[:, 0 : dims_of[1][1], :]
     wides[1]["over"][middle] = over
-    spread("raw", 2, WAYS[2], [wides[2][name] for name in WIDE_NAMES[:4]])
-    _, over, _ = wide_diag(2, slice(0, wides[2]["a"].shape[0]))
-    wides[2]["over"][...] = over
-    wide_coefs(2)
     finish_half(0, 1, False)
     kept[0][...] = pad[1 : 1 + nx, ROW : ROW + ny, :]
     stores[0].start()
@@ -552,6 +549,10 @@
 
     spread("raw", 1, CORNERS, [wides[1][name] for name in WIDE_NAMES[:4]])
     wide_coefs(1)
+    spread("raw", 2, WAYS[2], [wides[2][name] for name in WIDE_NAMES[:4]])
+    _, over, _ = wide_diag(2, slice(0, wides[2]["a"].shape[0]))
+    wides[2]["over"][...] = over
+    wide_coefs(2)
     u = wide_smooth(1)
     ny = dims_of[1][1]
     kept[1][...] = u[1:-1, 0:ny, :]

time: 28.8 us -> 28.7 us (level)
  no operation moved by 1% of the time
where the time goes in v6:
time: 28.7 us; the launch traced here: 28.6 us
  Pallas kernels  27.9 us (97%)
  between operations  0.64 us (2%)
    pallas_call x1, Pallas kernels, shards(): pl.pallas_call(functools.partial(kernel, dims_of, keys), out_shape=[jax.S...  26.3 us
    pallas_call x1, Pallas kernels, shards(): pl.pallas_call(store, out_shape=[jax.ShapeDtypeStruct(dims, jnp.float32)...  1.62 us

profile of v6, /device:TPU:0, one launch (start us, length us, event | category | flops | bytes accessed | tf_op | source)
XLA Modules:
  0.0 28.6 jit_solution(15641391972016423611)
XLA Ops:
  0.6 26.3 %vcycle.1 = (f32[8,8,512]{2,1,0:T(8,128)}, f32[4,4,256]{2,1,0:T(4,128)}, f32[2,2,128]{2,1,0:T(2,128)}) custom-call(f32[8,8,512]{2,1,0:T(8,128)} %refs_0_.1, f32[8,8,512]{2,1,0:T(8,128)} %refs_1_.1, bf16[8,8,512]{2,1,0:T(8,128)(2,1)} %refs_2_.1, bf16[8,8,512]{2,1,0:T(8,128)(2,1)} %refs_3_.1, bf16[8,8,512]{2,1,0:T(8,128)(2,1)} %refs_4_.1, ...), custom_call_target="tpu_custom_call" | custom-call | tf_op jit(solution)/shard_map/vcycle/pallas_call | solution.py:624
  27.0 1.6 %store.1 = (f32[8,8,512]{2,1,0:T(8,128)}, f32[4,4,256]{2,1,0:T(4,128)}, f32[2,2,128]{2,1,0:T(2,128)}) custom-call(f32[8,8,512]{2,1,0:T(8,128)} %get-tuple-element.6.refs_0_, f32[4,4,256]{2,1,0:T(4,128)} %get-tuple-element.7.refs_1_, f32[2,2,128]{2,1,0:T(2,128)} %get-tuple-element.8.refs_2_), custom_call_target="tpu_custom_call" | custom-call | tf_op jit(solution)/shard_map/store/pallas_call | solution.py:635

commit v7 on v6

--- a/solution.py
+++ b/solution.py
@@ -333,30 +333,40 @@
                 )
         send(group_of("toward", level) + group_of("ends", level))
 
-    def sums(level, pad):
-        these = per[level]
-        nx, ny, nz = dims_of[level]
-        own = pad[1 : 1 + nx, ROW : ROW + ny, :]
-        total = these["g"][...]
-        total = total + these["xu"][...] * pad[2 : 2 + nx, ROW : ROW + ny, :]
-        total = total + these["xl"][...] * pad[0:nx, ROW : ROW + ny, :]
-        total = total + these["yu"][...] * pad[1 : 1 + nx, ROW + 1 : ROW + 1 + ny, :]
-        total = total + these["yl"][...] * pad[1 : 1 + nx, ROW - 1 : ROW - 1 + ny, :]
-        total = total + these["zu"][...] * pltpu.roll(own, nz - 1, 2)
-        total = total + these["zl"][...] * pltpu.roll(own, 1, 2)
-        return own, total
-
-    def half_sweep(level, half, red):
+    def planes(pad, write):
+        these = per[0]
+        nx, ny, nz = dims_of[0]
+        rows, below, above = (slice(ROW + n, ROW + n + ny) for n in (0, -1, 1))
+
+        def step(x, carry):
+            here, low, high = pl.ds(x, 1), pl.ds(x + 1, 1), pl.ds(x + 2, 1)
+            own = pad[low, rows, :]
+            total = these["g"][here] + these["xu"][here] * pad[high, rows, :]
+            total = total + these["xl"][here] * pad[here, rows, :]
+            total = total + these["yu"][here] * pad[low, above, :]
+            total = total + these["yl"][here] * pad[low, below, :]
+            total = total + these["zu"][here] * pltpu.roll(own, nz - 1, 2)
+            total = total + these["zl"][here] * pltpu.roll(own, 1, 2)
+            write(x, own, total, jnp.logical_not(parity_at((1, ny, nz), x)))
+            return carry
+
+        lax.fori_loop(0, nx, step, 0, unroll=2)
+
+    def colour_step(source, target, colour):
+        def write(x, own, total, red):
+            new = jnp.where(red, total, own) if colour == 0 else jnp.where(red, own, total)
+            target[pl.ds(x + 1, 1), ROW : ROW + dims_of[0][1], :] = new
+
+        planes(source, write)
+
+    def half_sweep(level, half):
         these = per[level]
         dims = dims_of[level]
         nx, ny, nz = dims
         shut, pad = these["shut"], these["open"]
         kind = "half%d" % half
-        black = parity_at(dims)
-        shut[1 : 1 + nx, ROW : ROW + ny, :] = red
-        _, total = sums(level, shut)
-        value = jnp.where(black, total, red)
-        pad[1 : 1 + nx, ROW : ROW + ny, :] = value
+        colour_step(pad, shut, 0)
+        colour_step(shut, pad, 1)
         group = group_of(kind, level)
         for key in group:
             xs, ys = at_side(dims, key[2])
@@ -510,7 +520,6 @@
     nx, ny, nz = dims
     these = per[0]
     pad = these["open"]
-    red_cells = jnp.logical_not(parity_at(dims))
     coarse_coefs(0)
     put_raw(1)
     send([key for key in group_of("raw", 1) if key[2] in FACES])
@@ -523,15 +532,13 @@
     for way in FACES:
         hx, hy = halo_place(dims, way)
         pad[hx, hy, :] = in_buf[("first", 0, (-way[0], -way[1]))][...]
-    own, total = sums(0, pad)
-    half_sweep(0, 0, jnp.where(red_cells, total, own))
+    half_sweep(0, 0)
     send([key for key in group_of("raw", 1) if key[2] in CORNERS])
     coarse_coefs(1)
     put_raw(2)
     wide_start(2)
     finish_half(0, 0, False)
-    own, total = sums(0, pad)
-    half_sweep(0, 1, jnp.where(red_cells, total, own))
+    half_sweep(0, 1)
     send(group_of("raw", 2))
     spread("raw", 1, FACES, [wides[1][name] for name in WIDE_NAMES[:4]])
     middle = slice(REACH[1], REACH[1] + dims_of[1][0])
@@ -542,8 +549,12 @@
     finish_half(0, 1, False)
     kept[0][...] = pad[1 : 1 + nx, ROW : ROW + ny, :]
     stores[0].start()
-    own, total = sums(0, pad)
-    these["a"][...] = jnp.where(red_cells, these["diag"][...] * (total - own), 0.0)
+
+    def write(x, own, total, red):
+        here = pl.ds(x, 1)
+        these["a"][here] = jnp.where(red, these["diag"][here] * (total - own), 0.0)
+
+    planes(pad, write)
     take = functools.partial(lambda ref, i: ref[i : i + 1], these["a"])
     wide_send(1, squeeze(0, [take], (None,))[0])
 

time: 28.7 us -> 29.7 us (1.035)
  Pallas kernels: 27.9 us -> 28.9 us
    pallas_call x1, Pallas kernels: 26.3 us -> 27.3 us  [shards(): pl.pallas_call(functools.partial(kernel, dims_of, keys), out_shape=[jax.S...]
where the time goes in v7:
time: 29.7 us; the launch traced here: 29.6 us
  Pallas kernels  28.9 us (97%)
  between operations  0.64 us (2%)
    pallas_call x1, Pallas kernels, shards(): pl.pallas_call(functools.partial(kernel, dims_of, keys), out_shape=[jax.S...  27.3 us
    pallas_call x1, Pallas kernels, shards(): pl.pallas_call(store, out_shape=[jax.ShapeDtypeStruct(dims, jnp.float32)...  1.62 us

profile of v7, /device:TPU:0, one launch (start us, length us, event | category | flops | bytes accessed | tf_op | source)
XLA Modules:
  0.0 29.6 jit_solution(3961467728874708853)
XLA Ops:
  0.6 27.3 %vcycle.1 = (f32[8,8,512]{2,1,0:T(8,128)}, f32[4,4,256]{2,1,0:T(4,128)}, f32[2,2,128]{2,1,0:T(2,128)}) custom-call(f32[8,8,512]{2,1,0:T(8,128)} %refs_0_.1, f32[8,8,512]{2,1,0:T(8,128)} %refs_1_.1, bf16[8,8,512]{2,1,0:T(8,128)(2,1)} %refs_2_.1, bf16[8,8,512]{2,1,0:T(8,128)(2,1)} %refs_3_.1, bf16[8,8,512]{2,1,0:T(8,128)(2,1)} %refs_4_.1, ...), custom_call_target="tpu_custom_call" | custom-call | tf_op jit(solution)/shard_map/vcycle/pallas_call | solution.py:635
  27.9 1.6 %store.1 = (f32[8,8,512]{2,1,0:T(8,128)}, f32[4,4,256]{2,1,0:T(4,128)}, f32[2,2,128]{2,1,0:T(2,128)}) custom-call(f32[8,8,512]{2,1,0:T(8,128)} %get-tuple-element.6.refs_0_, f32[4,4,256]{2,1,0:T(4,128)} %get-tuple-element.7.refs_1_, f32[2,2,128]{2,1,0:T(2,128)} %get-tuple-element.8.refs_2_), custom_call_target="tpu_custom_call" | custom-call | tf_op jit(solution)/shard_map/store/pallas_call | solution.py:646
